TPU v7x, 256 devices: a whole 4x4x8 slice. The times are simulated.
256 devices in a mesh: seq: 128 (over y, z, x_lo, core), head: 2 (over x_hi).
Axes of the slice: x: 4 (x_hi: 2, x_lo: 2; x = x_hi * 2 + x_lo), y: 4, z: 8, core: 2. Of those that a mesh axis runs over, the one named last changes fastest.
Arguments:
- queries: bfloat16 [16384, 4096], P('seq', 'head'), may hold values from -36 to 36
- keys: bfloat16 [16384, 1024], P('seq', 'head'), may hold values from -7.5 to 7.5
- values: bfloat16 [16384, 1024], P('seq', 'head'), may hold values from -16 to 16
- windows: int32 [32], P('head'), may hold values from 64 to 256, as said below
- out_weight: bfloat16 [4096, 4096], P('head', 'seq'), may hold values from -0.09375 to 0.09375
- grad_out: bfloat16 [16384, 4096], P('seq', 'head'), may hold values from -6 to 6
Outputs:
- output: bfloat16 [16384, 4096], P('seq', 'head')
- grad_queries: bfloat16 [16384, 4096], P('seq', 'head')
- grad_keys: bfloat16 [16384, 1024], P('seq', 'head')
- grad_values: bfloat16 [16384, 1024], P('seq', 'head')
Inputs may be any that keep to these rules, and one draw needn't show every extreme that they name: windows[h] counts the latest positions, the query's own included, that query head h attends besides the first 4 tokens.
All inputs are finite; a program needn't handle non-finite values.
Results may differ from a plain program's by a relative error of at most 0.034.
Values may be sent and summed in bfloat16 or wider, within the bound.
A program may use at most 64 MiB of HBM per device.

v0:
```python
import math

import jax
import jax.numpy as jnp
from jax import lax
from jax.sharding import PartitionSpec as P

HEAD_DIM = 128
SINKS = 4


MASKED_SCORE = -1e30


def from_root(x, axis, root):
    mine = lax.axis_index(axis) == root
    return lax.psum(jnp.where(mine, x, jnp.zeros_like(x)), axis)


def from_behind(block, axis, distance):
    devices = range(lax.axis_size(axis))
    route = [(i - distance, i) for i in devices if i - distance in devices]
    return lax.ppermute(block, axis, route)


def head_masks(head_windows, positions):
    query_pos, key_pos, sink_pos = positions
    distance = query_pos[:, None] - key_pos[None, :]
    inside = (distance >= 0) & (key_pos[None, :] >= SINKS)
    in_window = distance[None] < head_windows[:, None, None]
    band_mask = inside[None] & in_window
    sink_mask = (sink_pos[None, :] <= query_pos[:, None])[None]
    return (band_mask, sink_mask)


def head_scores(query_heads, band_keys, sink_keys, band_mask, sink_mask):
    score_scale = 1.0 / math.sqrt(HEAD_DIM)
    band_scores = (
        jnp.einsum("gtd,jd->gtj", query_heads, band_keys, preferred_element_type=jnp.float32)
        * score_scale
    )
    sink_scores = (
        jnp.einsum("gtd,sd->gts", query_heads, sink_keys, preferred_element_type=jnp.float32)
        * score_scale
    )
    return (
        jnp.where(band_mask, band_scores, MASKED_SCORE),
        jnp.where(sink_mask, sink_scores, MASKED_SCORE),
    )


def forward_head(
    query_heads, band_keys, band_values, sink_keys, sink_values, head_windows, positions
):
    band_mask, sink_mask = head_masks(head_windows, positions)
    band_scores, sink_scores = head_scores(query_heads, band_keys, sink_keys, band_mask, sink_mask)
    row_max = jnp.maximum(band_scores.max(-1), sink_scores.max(-1))
    totals = jnp.exp(band_scores - row_max[..., None]).sum(-1) + jnp.exp(
        sink_scores - row_max[..., None]
    ).sum(-1)
    log_total = row_max + jnp.log(totals)
    band_probs = jnp.where(band_mask, jnp.exp(band_scores - log_total[..., None]), 0.0).astype(
        jnp.bfloat16
    )
    sink_probs = jnp.where(sink_mask, jnp.exp(sink_scores - log_total[..., None]), 0.0).astype(
        jnp.bfloat16
    )
    attn = jnp.einsum("gtj,jd->gtd", band_probs, band_values, preferred_element_type=jnp.float32)
    attn = attn + jnp.einsum(
        "gts,sd->gtd", sink_probs, sink_values, preferred_element_type=jnp.float32
    )
    return (attn.astype(jnp.bfloat16), log_total)


def backward_head(
    query_heads,
    band_keys,
    band_values,
    sink_keys,
    sink_values,
    head_windows,
    log_total,
    attn_head,
    grad_head,
    positions,
):
    band_mask, sink_mask = head_masks(head_windows, positions)
    band_scores, sink_scores = head_scores(query_heads, band_keys, sink_keys, band_mask, sink_mask)
    band_probs = jnp.where(band_mask, jnp.exp(band_scores - log_total[..., None]), 0.0)
    sink_probs = jnp.where(sink_mask, jnp.exp(sink_scores - log_total[..., None]), 0.0)
    delta = jnp.sum(grad_head.astype(jnp.float32) * attn_head.astype(jnp.float32), -1)
    band_dprobs = jnp.einsum(
        "gtd,jd->gtj", grad_head, band_values, preferred_element_type=jnp.float32
    )
    sink_dprobs = jnp.einsum(
        "gtd,sd->gts", grad_head, sink_values, preferred_element_type=jnp.float32
    )
    score_scale = 1.0 / math.sqrt(HEAD_DIM)
    band_dscores = (band_probs * (band_dprobs - delta[..., None]) * score_scale).astype(
        jnp.bfloat16
    )
    sink_dscores = (sink_probs * (sink_dprobs - delta[..., None]) * score_scale).astype(
        jnp.bfloat16
    )
    grad_query = jnp.einsum(
        "gtj,jd->gtd", band_dscores, band_keys, preferred_element_type=jnp.float32
    )
    grad_query = grad_query + jnp.einsum(
        "gts,sd->gtd", sink_dscores, sink_keys, preferred_element_type=jnp.float32
    )
    band_low = band_probs.astype(jnp.bfloat16)
    sink_low = sink_probs.astype(jnp.bfloat16)
    band_key_grads = jnp.einsum(
        "gtj,gtd->jd", band_dscores, query_heads, preferred_element_type=jnp.float32
    )
    band_value_grads = jnp.einsum(
        "gtj,gtd->jd", band_low, grad_head, preferred_element_type=jnp.float32
    )
    sink_key_grads = jnp.einsum(
        "gts,gtd->sd", sink_dscores, query_heads, preferred_element_type=jnp.float32
    )
    sink_value_grads = jnp.einsum(
        "gts,gtd->sd", sink_low, grad_head, preferred_element_type=jnp.float32
    )
    return (
        grad_query.astype(jnp.bfloat16),
        band_key_grads,
        band_value_grads,
        sink_key_grads,
        sink_value_grads,
    )


def merge_heads(array):
    return array.transpose(1, 0, 2).reshape(array.shape[1], -1)


def local(queries, keys, values, windows, out_weight, grad_out):
    slab_rows = queries.shape[0]
    q_heads = windows.shape[0]
    kv_heads = keys.shape[1] // HEAD_DIM
    group_size = q_heads // kv_heads
    seq_index = lax.axis_index("seq")
    first_row = seq_index * slab_rows
    band_start = first_row - 2 * slab_rows
    positions = (
        first_row + jnp.arange(slab_rows, dtype=jnp.int32),
        band_start + jnp.arange(3 * slab_rows, dtype=jnp.int32),
        jnp.arange(SINKS, dtype=jnp.int32),
    )

    def split_heads(array, row_count):
        return array.reshape(row_count, kv_heads, HEAD_DIM).transpose(1, 0, 2)

    def to_heads(array):
        return array.reshape(slab_rows, kv_heads, group_size, HEAD_DIM).transpose(1, 2, 0, 3)

    def from_heads(array):
        return array.transpose(2, 0, 1, 3).reshape(slab_rows, q_heads * HEAD_DIM)

    sink_pair = from_root(jnp.stack([keys[:SINKS], values[:SINKS]]), "seq", 0)
    own_pair = jnp.stack([keys, values])
    near_pair = from_behind(own_pair, "seq", 1)
    far_pair = from_behind(own_pair, "seq", 2)
    band_pair = jnp.concatenate([far_pair, near_pair, own_pair], axis=1)
    band_keys = split_heads(band_pair[0], 3 * slab_rows)
    band_values = split_heads(band_pair[1], 3 * slab_rows)
    sink_keys = split_heads(sink_pair[0], SINKS)
    sink_values = split_heads(sink_pair[1], SINKS)
    query_heads = to_heads(queries)
    head_windows = windows.reshape(kv_heads, group_size)
    grad_full = lax.all_gather(grad_out, "head", axis=1, tiled=True)

    def forward_item(items):
        return forward_head(*items, positions)

    attn_heads, log_total = lax.map(
        forward_item, (query_heads, band_keys, band_values, sink_keys, sink_values, head_windows)
    )
    attn_all = from_heads(attn_heads)
    weights_piece = lax.all_gather(out_weight, "seq", axis=1, tiled=True)
    out_running = jnp.dot(attn_all, weights_piece, preferred_element_type=jnp.float32)
    grad_sum = lax.dot_general(
        grad_full, weights_piece, (((1,), (1,)), ((), ())), preferred_element_type=jnp.float32
    )
    output = lax.psum_scatter(
        out_running.astype(jnp.bfloat16), "head", scatter_dimension=1, tiled=True
    )
    grad_heads = to_heads(grad_sum.astype(jnp.bfloat16))

    def backward_item(items):
        return backward_head(*items, positions)

    grad_query, band_key_grads, band_value_grads, sink_key_grads, sink_value_grads = lax.map(
        backward_item,
        (
            query_heads,
            band_keys,
            band_values,
            sink_keys,
            sink_values,
            head_windows,
            log_total,
            attn_heads,
            grad_heads,
        ),
    )
    partials = jnp.stack([merge_heads(band_key_grads), merge_heads(band_value_grads)])
    far_part = partials[:, :slab_rows]
    near_part = partials[:, slab_rows : 2 * slab_rows]
    own_part = partials[:, 2 * slab_rows :]
    from_next = from_behind(near_part.astype(jnp.bfloat16), "seq", -1).astype(near_part.dtype)
    from_after = from_behind(far_part.astype(jnp.bfloat16), "seq", -2).astype(far_part.dtype)
    totals = own_part + from_next + from_after
    sink_part = jnp.stack([merge_heads(sink_key_grads), merge_heads(sink_value_grads)])
    sink_total = lax.psum(sink_part, "seq")
    root_sums = jnp.where(seq_index == 0, sink_total, 0.0)
    totals = totals.at[:, :SINKS].add(root_sums)
    return (
        output,
        from_heads(grad_query),
        totals[0].astype(jnp.bfloat16),
        totals[1].astype(jnp.bfloat16),
    )


def solution(mesh):
    in_specs = (
        P("seq", "head"),
        P("seq", "head"),
        P("seq", "head"),
        P("head"),
        P("head", "seq"),
        P("seq", "head"),
    )
    out_specs = (P("seq", "head"), P("seq", "head"), P("seq", "head"), P("seq", "head"))
    return jax.shard_map(local, mesh=mesh, in_specs=in_specs, out_specs=out_specs, check_vma=False)
```

profile of v0, /device:TPU:4, one launch (start us, length us, event | category | flops | bytes accessed | tf_op | source)
XLA Modules:
  0.0 918.2 jit_solution(11983895323066897548)
XLA Ops:
  8.7 1.0 copy.21
  9.7 1.0 copy.22
  10.8 1.8 collective-permute-start.1
  12.6 3.3 collective-permute-start
  15.9 0.7 slice_bitcast_fusion.4
  17.3 287.8 %psum.14 = bf16[2,4,512]{2,1,0:T(4,128)(2,1)S(1)} all-reduce(bf16[2,4,512]{2,1,0:T(4,128)(2,1)S(1)} %maximum_select_fusion), channel_id=1, replica_groups=mesh['seq'=128,'head'=2] {'seq'}, use_global_device_ids=true, to_apply=%region_0.1 | all-reduce | flops 4096 | bytes 16384 | tf_op jit(solution)/shard_map/psum | solution.py:17
  305.9 7.9 while.33
  314.1 8.4 convolution_convert_fusion.1
  323.1 12.5 %convolution_convert_fusion = bf16[128,4096]{1,0:T(8,128)(2,1)} fusion(bf16[128,2048]{0,1:T(8,128)(2,1)S(1)} %bitcast.229, bf16[2048,4096]{0,1:T(8,128)(2,1)} %all-gather.3.cloned.1.call-done), kind=kOutput, calls=%fused_computation.132 | convolution fusion | flops 2148007936 | bytes 18350080 | tf_op jit(solution)/shard_map/dot_general | solution.py:182
  335.7 17.4 %while.34 = (s32[]{:T(128)}, bf16[4,4,128,128]{3,2,1,0:T(8,128)(2,1)S(1)}, f32[4,384,128]{2,1,0:T(8,128)}, f32[4,384,128]{2,1,0:T(8,128)}, f32[4,4,128]{2,1,0:T(...) while((s32[]{:T(128)}, ...), condition=%wide.region_10.11_spmd.clone, body=%wide.region_8.10_spmd.clone.sunk | while | flops 257051904 | bytes 6761449 | solution.py:194
  337.5 1.0 fusion.195
  339.1 1.0 fusion.194
  341.9 1.0 fusion.195
  343.4 1.0 fusion.194
  346.2 1.0 fusion.195
  347.8 1.0 fusion.194
  350.6 1.0 fusion.195
  352.1 1.0 fusion.194
  353.1 0.8 copy-done
  353.9 1.7 copy.34
  357.1 1.3 collective-permute-start.2
  358.4 1.3 collective-permute-start.3
  360.1 1.2 reshape.306
  361.3 549.5 %psum.15 = f32[2,4,512]{2,1,0:T(4,128)S(1)} all-reduce(f32[2,4,512]{2,1,0:T(4,128)S(1)} %pad_maximum_fusion.1), channel_id=1, replica_groups=mesh['seq'=128,'head'=2] {'seq'}, use_global_device_ids=true, to_apply=%region_11.12 | all-reduce | flops 4096 | bytes 32768 | tf_op jit(solution)/shard_map/psum | solution.py:216
  (183 shorter events, 23.1 us)
Async XLA Ops:
  7.2 9.5 %copy-start.4 = (s32[16]{0:T(128)S(1)}, s32[16]{0:T(128)}, u32[]{:S(2)}) copy-start(s32[16]{0:T(128)} %param.15) | copy-start | bytes 196
  7.2 9.6 %copy-start.3 = (bf16[128,2048]{1,0:T(8,128)(2,1)S(1)}, bf16[128,2048]{1,0:T(8,128)(2,1)}, u32[]{:S(2)}) copy-start(bf16[128,2048]{1,0:T(8,128)(2,1)} %param.12) | copy-start | bytes 1572868
  7.2 306.9 %all-gather.5.cloned.1.call-start = ((), (), s32[]{:S(2)}) async-start(), calls=%async_computation.3 | async-start | bytes 1572864 | tf_op jit(solution)/shard_map/all_gather | solution.py:172
  7.9 306.2 %all-gather.3.cloned.1.call-start = ((), (), s32[]{:S(2)}) async-start(), calls=%async_computation.1 | async-start | bytes 16908288 | tf_op jit(solution)/shard_map/all_gather | solution.py:181
  8.7 903.0 %reduce-scatter.2.cloned.1.call-start = ((), (), s32[]{:S(2)}) async-start(), calls=%async_computation.2 | async-start | bytes 1572864 | tf_op jit(solution)/shard_map/reduce_scatter | solution.py:186
  10.8 294.3 %collective-permute-start.1 = (bf16[2,128,512]{1,2,0:T(8,128)(2,1)S(1)}, bf16[2,128,512]{1,2,0:T(8,128)(2,1)S(1)}, u32[]{:S(2)}, u32[]{:S(2)}) collective-permute-start(bf16[2,128,512]{1,2,0:T(8,128)(2,1)S(1)} %pad_maximum_fusion), channel_id=1, source_target_pairs={{0,2},{2,4},{4,6},{6,8},{8,10},{10,12},{12,14},{14,16},{16,18},{18... | collective-permute-start | bytes 786440 | tf_op jit(solution)/shard_map/ppermute | solution.py:23
  12.6 292.6 %collective-permute-start = (bf16[2,128,512]{1,2,0:T(8,128)(2,1)S(1)}, bf16[2,128,512]{1,2,0:T(8,128)(2,1)S(1)}, u32[]{:S(2)}, u32[]{:S(2)}) collective-permute-start(bf16[2,128,512]{1,2,0:T(8,128)(2,1)S(1)} %pad_maximum_fusion), channel_id=1, source_target_pairs={{0,4},{2,6},{4,8},{6,10},{8,12},{10,14},{12,16},{14,18},{16,20},{1... | collective-permute-start | bytes 786440 | tf_op jit(solution)/shard_map/ppermute | solution.py:23
  353.1 0.8 copy-start
  353.9 2.0 copy-start.2
  356.9 2.8 copy-start.1
  357.1 553.7 %collective-permute-start.2 = (bf16[2,128,512]{2,1,0:T(8,128)(2,1)S(1)}, bf16[2,128,512]{2,1,0:T(8,128)(2,1)S(1)}, u32[]{:S(2)}, u32[]{:S(2)}) collective-permute-start(bf16[2,128,512]{2,1,0:T(8,128)(2,1)S(1)} %get-tuple-element.340), channel_id=1, source_target_pairs={{2,0},{4,2},{6,4},{8,6},{10,8},{12,10},{14,12},{16,14},{18,16},{20... | collective-permute-start | bytes 786440 | tf_op jit(solution)/shard_map/ppermute | solution.py:23
  358.4 552.4 %collective-permute-start.3 = (bf16[2,128,512]{2,1,0:T(8,128)(2,1)S(1)}, bf16[2,128,512]{2,1,0:T(8,128)(2,1)S(1)}, u32[]{:S(2)}, u32[]{:S(2)}) collective-permute-start(bf16[2,128,512]{2,1,0:T(8,128)(2,1)S(1)} %get-tuple-element.341), channel_id=1, source_target_pairs={{4,0},{6,2},{8,4},{10,6},{12,8},{14,10},{16,12},{18,14},{20,16},{2... | collective-permute-start | bytes 786440 | tf_op jit(solution)/shard_map/ppermute | solution.py:23
Sparse Core Ops, SparseCore 0:
  9.8 28.7 all-gather.4
  40.5 231.9 all-gather.2
  335.7 17.8 reduce-scatter.1
where the time goes:
time: 919 us; the launch traced here: 918 us
  blocking collectives  837 us (91%)
  matrix products  41.5 us (5%)
  between operations  14.1 us (2%)
  local copies, waits for them, and re-layouts  11.2 us (1%)
    psum x1, blocking collectives, local(): sink_total = lax.psum(sink_part, 'seq')  549 us
    psum x1, blocking collectives, from_root(): return lax.psum(jnp.where(mine, x, jnp.zeros_like(x)), axis)  288 us
  transfers between devices with their start and end apart: 7, of which 0 were waited for; matrix products, arithmetic and copies ran while one was open for 4% of the time, Pallas kernels for 0%

commit v1 on v0

v1 whole, which is shorter than its diff:
```python
import functools
import math

import jax
import jax.numpy as jnp
from jax import lax
from jax.experimental import pallas as pl
from jax.experimental.pallas import tpu as pltpu
from jax.sharding import PartitionSpec as P

HEAD = 128
SINKS = 4
SLAB = 128
NY, NZ = 4, 8
MASKED = -1e30
FAR_AWAY = 1 << 20
MESH = pl.DeviceIdType.MESH
SCALE = 1.0 / math.sqrt(HEAD)
EXP2_SCALE = SCALE * math.log2(math.e)
Y_FIRST = (256, 256, 256, 128)
STAGES = 4


def dot(a, b, ca, cb):
    return lax.dot_general(a, b, (((ca,), (cb,)), ((), ())), preferred_element_type=jnp.float32)


class Links:
    def __init__(self, send_sems, recv_sems):
        self.send_sems, self.recv_sems = send_sems, recv_sems
        self.copies, self.arrived = {}, set()

    def start(self, name, src, dst, device):
        n = len(self.copies)
        copy = pltpu.make_async_remote_copy(
            src_ref=src,
            dst_ref=dst,
            send_sem=self.send_sems.at[n],
            recv_sem=self.recv_sems.at[n],
            device_id=device,
            device_id_type=MESH,
        )
        copy.start()
        self.copies[name] = copy

    def need(self, *names):
        for name in names:
            if name not in self.arrived:
                self.arrived.add(name)
                self.copies[name].wait_recv()

    def finish(self):
        self.need(*self.copies)
        for copy in self.copies.values():
            copy.wait_send()


def kernel(
    q_ref, k_ref, v_ref, win_ref, w_ref, go_ref,
    out_ref, gq_ref, gk_ref, gv_ref,
    G, kv, go_other, dist, probs, attn, ga, acc, out_send, out_recv, ds_buf, pl_buf, own,
    g_send, g_recv, sinks, sink_r1, sink_r2, sink_r3,
    send_sems, recv_sems, local_sems, tree_send, tree_recv,
):
    s, hd = lax.axis_index("seq"), lax.axis_index("head")
    c, x, z, y = s % 2, (s // 2) % 2, (s // 4) % NZ, s // (4 * NZ)
    n_seq = 4 * NY * NZ

    def at(y, z, x, c):
        return (((y * NZ + z) * 2 + x) * 2 + c, hd)

    def ym(k):
        return (y + k + NY) % NY

    def zm(k):
        return (z + k + NZ) % NZ

    y_dev = {k: at(ym(k), z, x, c) for k in (1, -1, 2)}
    z_dev = {k: at(y, zm(k), x, c) for k in (1, -1)}
    x_dev, sib, pair = at(y, z, 1 - x, c), at(y, z, x, 1 - c), (s, 1 - hd)
    after1, after2 = ((s + 1) % n_seq, hd), ((s + 2) % n_seq, hd)
    before1, before2 = ((s + n_seq - 1) % n_seq, hd), ((s + n_seq - 2) % n_seq, hd)
    quad = 2 * x + c
    leader = quad == 0
    column_leader = leader & (z == 0)
    root = column_leader & (y == 0)

    barrier = pltpu.get_barrier_semaphore()

    def hello(device):
        pl.semaphore_signal(barrier, inc=1, device_id=device, device_id_type=MESH)

    everyone = [y_dev[1], y_dev[-1], y_dev[2], z_dev[1], z_dev[-1], x_dev, sib, pair,
                after1, after2, before1, before2]
    for device in everyone:
        hello(device)

    @pl.when(leader)
    def _():
        for k in range(1, 4):
            hello(at(y, z, k // 2, k % 2))

    @pl.when(column_leader)
    def _():
        for k in range(1, NZ):
            hello(at(y, k, 0, 0))

    @pl.when(root)
    def _():
        for k in range(1, NY):
            hello(at(k, 0, 0, 0))

    @pl.when(quad != 0)
    def _():
        hello(at(y, z, 0, 0))

    @pl.when(leader & (z != 0))
    def _():
        hello(at(y, 0, 0, 0))

    @pl.when(column_leader & (y != 0))
    def _():
        hello(at(0, 0, 0, 0))

    tree_peers = jnp.where(quad != 0, 1, 3 + jnp.where(z != 0, 1, NZ - 1 + jnp.where(y != 0, 1, NY - 1)))
    pl.semaphore_wait(barrier, len(everyone) + tree_peers)

    links = Links(send_sems, recv_sems)
    start, need = links.start, links.need

    locals_ = []
    for h in range(STAGES):
        piece = w_ref.at[:, pl.ds(h * 512, 512)]
        mine = G.at[h, y, z, x, c]
        copy = pltpu.make_async_copy(piece, mine, local_sems.at[h])
        copy.start()
        locals_.append(copy)
        start(("x", h), piece, mine, x_dev)

    kv[0, 2 * SLAB : 3 * SLAB, :] = k_ref[...]
    kv[1, 2 * SLAB : 3 * SLAB, :] = v_ref[...]
    kv[:, 3 * SLAB + 16 :, :] = jnp.zeros((2, SLAB - 16, 512), jnp.bfloat16)
    own_kv = kv.at[:, pl.ds(2 * SLAB, SLAB)]
    first16 = kv.at[:, pl.ds(2 * SLAB, 16)]
    sink_kv = kv.at[:, pl.ds(3 * SLAB, 16)]

    def tree_copy(src, slot, rslot, device):
        return pltpu.make_async_remote_copy(
            src_ref=src, dst_ref=sink_kv, send_sem=tree_send.at[slot], recv_sem=tree_recv.at[rslot],
            device_id=device, device_id_type=MESH)

    def spread():
        @pl.when(root)
        def _():
            kv[:, 3 * SLAB : 3 * SLAB + 16, :] = kv[:, 2 * SLAB : 2 * SLAB + 16, :]
            for k in range(1, NY):
                tree_copy(first16, k, 0, at(k, 0, 0, 0)).start()

        @pl.when(column_leader & (y != 0))
        def _():
            tree_copy(first16, 0, 0, sib).wait_recv()

        @pl.when(column_leader)
        def _():
            for k in range(1, NZ):
                tree_copy(sink_kv, 3 + k, 0, at(y, k, 0, 0)).start()

        @pl.when(leader & (z != 0))
        def _():
            tree_copy(first16, 0, 0, sib).wait_recv()

        @pl.when(leader)
        def _():
            for k in range(1, 4):
                tree_copy(sink_kv, 10 + k, 0, at(y, z, k // 2, k % 2)).start()

        @pl.when(quad != 0)
        def _():
            tree_copy(first16, 0, 0, sib).wait_recv()

        @pl.when(leader)
        def _():
            for k in range(1, 4):
                tree_copy(sink_kv, 10 + k, 0, at(y, z, k // 2, k % 2)).wait_send()

        @pl.when(column_leader)
        def _():
            for k in range(1, NZ):
                tree_copy(sink_kv, 3 + k, 0, at(y, k, 0, 0)).wait_send()

        @pl.when(root)
        def _():
            for k in range(1, NY):
                tree_copy(first16, k, 0, at(k, 0, 0, 0)).wait_send()

    start("near", own_kv, kv.at[:, pl.ds(SLAB, SLAB)], after1)
    start("far", own_kv, kv.at[:, pl.ds(0, SLAB)], after2)
    start("go", go_ref, go_other, pair)

    def lanes(h, first):
        return pl.ds(0, Y_FIRST[h]) if first else pl.ds(Y_FIRST[h], 512 - Y_FIRST[h])

    def block(h, first, ys, zs, xs=pl.ds(0, 2)):
        return G.at[h, ys, zs, xs, c, :, lanes(h, first)]

    one = lambda i: pl.ds(i, 1)
    all_y, all_z = pl.ds(0, NY), pl.ds(0, NZ)
    z_half = {1: pl.ds(0, NZ // 2), -1: pl.ds(NZ // 2, NZ // 2)}
    y_half = {1: pl.ds(0, NY // 2), -1: pl.ds(NY // 2, NY // 2)}

    def push(name, ref, device):
        start(name, ref, ref, device)

    def Ay(h):
        locals_[h].wait()
        need(("x", h))
        for k in (1, -1, 2):
            push(("Ay", h, k), block(h, True, one(y), one(z)), y_dev[k])

    def Az(h, k):
        if k == 1:
            need(*[("Ay", h, j) for j in (1, -1, 2)])
            push(("sA0", h), block(h, True, all_y, one(z)), sib)
        for d in (1, -1):
            ref = block(h, True, all_y, one(zm(-d * (k - 1))))
            if k > 1:
                need(("Az", h, k - 1, d))
                push(("sAz", h, k - 1, d), ref, sib)
            if k == 4:
                ref = block(h, True, y_half[d], one(zm(-d * 3)))
            push(("Az", h, k, d), ref, z_dev[d])

    def Aend(h):
        need(("Az", h, 4, 1), ("Az", h, 4, -1))
        push(("sA4", h), block(h, True, all_y, one(zm(4))), sib)

    def Bz(h, k):
        for d in (1, -1):
            if k > 1:
                need(("Bz", h, k - 1, d))
            xs = pl.ds(0, 2) if k < 4 else pl.ds(0 if d == 1 else 1, 1)
            push(("Bz", h, k, d), block(h, False, one(y), one(zm(-d * (k - 1))), xs), z_dev[d])

    def By(h):
        need(("Bz", h, 4, 1), ("Bz", h, 4, -1))
        for which in (1, -1):
            for d in (1, -1):
                push(("By", h, d, which), block(h, False, one(y), z_half[d * which]), y_dev[d])
        push(("sB0", h), block(h, False, one(y), all_z), sib)

    def By2(h):
        for d in (1, -1):
            need(("By", h, d, 1))
            ref = block(h, False, one(ym(-d)), z_half[d])
            push(("By2", h, d), ref, y_dev[d])
            push(("sBy", h, d, 1), ref, sib)

    def Bend(h):
        for d in (1, -1):
            need(("By", h, d, -1))
            push(("sBy", h, d, -1), block(h, False, one(ym(-d)), z_half[-d]), sib)
        need(("By2", h, 1), ("By2", h, -1))
        push(("sB2", h), block(h, False, one(ym(2)), all_z), sib)

    def gathered(h):
        names = [("sA0", h), ("sA4", h), ("sB0", h), ("sB2", h)]
        names += [("sAz", h, k, d) for k in (1, 2, 3) for d in (1, -1)]
        names += [("sBy", h, d, w) for d in (1, -1) for w in (1, -1)]
        need(*names)

    def masks():
        row = lax.broadcasted_iota(jnp.int32, (SLAB, 4 * SLAB), 0)
        col = lax.broadcasted_iota(jnp.int32, (SLAB, 4 * SLAB), 1)
        first = s * SLAB
        gap = row - col + 2 * SLAB
        band = (col < 3 * SLAB) & (gap >= 0) & (first - 2 * SLAB + col >= SINKS)
        place = col - 3 * SLAB
        sink = (place >= 0) & (place < SINKS) & (place <= first + row)
        dist[...] = jnp.where(band, gap, jnp.where(sink, 0, FAR_AWAY))

    def forward(h):
        keys, vals = kv[0, :, h * HEAD : (h + 1) * HEAD], kv[1, :, h * HEAD : (h + 1) * HEAD]
        for j in range(4 * h, 4 * h + 4):
            cols = slice(j * HEAD, (j + 1) * HEAD)
            scores = dot(q_ref[:, cols], keys, 1, 1)
            scores = jnp.where(dist[...] < win_ref[j], scores, MASKED)
            top = jnp.max(scores, axis=1, keepdims=True)
            p = jnp.exp2((scores - top) * EXP2_SCALE)
            p = p * (1.0 / jnp.sum(p, axis=1, keepdims=True))
            probs[j] = p
            attn[:, cols] = dot(p.astype(jnp.bfloat16), vals, 1, 0).astype(jnp.bfloat16)

    def project(h, half):
        rows = slice(h * 512, (h + 1) * 512)
        for k in range(4):
            yy = 2 * (hd if half == 0 else 1 - hd) + k // 2
            w = G[h, yy, (k % 2) * 4 : (k % 2) * 4 + 4].reshape(512, 512)
            cols = slice(k * 512, (k + 1) * 512)
            o = dot(attn[:, rows], w, 1, 1)
            if h > 0:
                o = o + acc[half, :, cols]
            if h == STAGES - 1 and half == 1:
                out_send[k] = o.astype(jnp.bfloat16)
                start(("out", k), out_send.at[k], out_recv.at[k], pair)
            else:
                acc[half, :, cols] = o
            g = dot((go_ref if half == 0 else go_other)[:, cols], w, 1, 0)
            if half == 1 and k == 0:
                ga[...] = g
            else:
                ga[...] += g

    def backward(h):
        keys, vals = kv[0, :, h * HEAD : (h + 1) * HEAD], kv[1, :, h * HEAD : (h + 1) * HEAD]
        for i in range(4):
            j = 4 * h + i
            cols = slice(j * HEAD, (j + 1) * HEAD)
            g = ga[:, i * HEAD : (i + 1) * HEAD].astype(jnp.bfloat16)
            delta = jnp.sum(
                g.astype(jnp.float32) * attn[:, cols].astype(jnp.float32), axis=1, keepdims=True
            )
            p = probs[j]
            ds = (p * (dot(g, vals, 1, 1) - delta) * SCALE).astype(jnp.bfloat16)
            gq_ref[:, cols] = dot(ds, keys, 1, 0).astype(jnp.bfloat16)
            ds_buf[i * SLAB : (i + 1) * SLAB, :] = ds
            pl_buf[i * SLAB : (i + 1) * SLAB, :] = p.astype(jnp.bfloat16)
        g4 = jnp.concatenate([ga[:, i * HEAD : (i + 1) * HEAD] for i in range(4)], axis=0)
        q4 = jnp.concatenate(
            [q_ref[:, (4 * h + i) * HEAD : (4 * h + i + 1) * HEAD] for i in range(4)], axis=0
        )
        lane = slice(h * HEAD, (h + 1) * HEAD)
        dk = dot(ds_buf[...], q4, 0, 0)
        dv = dot(pl_buf[...], g4.astype(jnp.bfloat16), 0, 0)
        for i, d in enumerate((dk, dv)):
            g_send[h, 0, i] = d[:SLAB].astype(jnp.bfloat16)
            g_send[h, 1, i] = d[SLAB : 2 * SLAB].astype(jnp.bfloat16)
            own[i, :, lane] = d[2 * SLAB : 3 * SLAB]
            sinks[i * 8 : i * 8 + 8, lane] = d[3 * SLAB : 3 * SLAB + 8]
        start(("gfar", h), g_send.at[h, 0], g_recv.at[h, 0], before2)
        start(("gnear", h), g_send.at[h, 1], g_recv.at[h, 1], before1)

    def up(dst, sem, slot, device):
        return pltpu.make_async_remote_copy(
            src_ref=sinks, dst_ref=dst, send_sem=tree_send.at[14], recv_sem=tree_recv.at[sem + slot],
            device_id=device, device_id_type=MESH)

    def collect():
        @pl.when(quad != 0)
        def _():
            copy = up(sink_r1.at[quad - 1], 1, quad - 1, at(y, z, 0, 0))
            copy.start()
            copy.wait_send()

        @pl.when(leader)
        def _():
            for k in range(3):
                up(sink_r1.at[k], 1, k, sib).wait_recv()
            sinks[...] = sinks[...] + sink_r1[0] + sink_r1[1] + sink_r1[2]

            @pl.when(z != 0)
            def _():
                copy = up(sink_r2.at[z - 1], 4, z - 1, at(y, 0, 0, 0))
                copy.start()
                copy.wait_send()

            @pl.when(z == 0)
            def _():
                total = sinks[...]
                for k in range(NZ - 1):
                    up(sink_r2.at[k], 4, k, sib).wait_recv()
                    total = total + sink_r2[k]
                sinks[...] = total

                @pl.when(y != 0)
                def _():
                    copy = up(sink_r3.at[y - 1], 11, y - 1, at(0, 0, 0, 0))
                    copy.start()
                    copy.wait_send()

                @pl.when(y == 0)
                def _():
                    total = sinks[...]
                    for k in range(NY - 1):
                        up(sink_r3.at[k], 11, k, sib).wait_recv()
                        total = total + sink_r3[k]
                    keep = lax.broadcasted_iota(jnp.int32, (8, 512), 0) < SINKS
                    for i in range(2):
                        own[i, 0:8, :] = own[i, 0:8, :] + jnp.where(
                            keep, total[i * 8 : i * 8 + 8], 0.0
                        )

    Ay(0)
    Bz(0, 1)
    Ay(1)
    masks()
    spread()
    Bz(0, 2)
    Az(0, 1)
    Bz(1, 1)
    need("near", "far")
    Bz(0, 3)
    Az(0, 2)
    Bz(1, 2)
    forward(0)
    Bz(0, 4)
    Az(0, 3)
    Bz(1, 3)
    forward(1)
    By(0)
    Az(0, 4)
    Bz(1, 4)
    forward(2)
    Aend(0)
    Az(1, 1)
    Ay(2)
    By2(0)
    By(1)
    forward(3)
    Bz(2, 1)
    Az(1, 2)
    Bend(0)
    need("go")
    Bz(2, 2)
    Az(1, 3)
    gathered(0)
    project(0, 1)
    Bz(2, 3)
    Az(1, 4)
    By2(1)
    project(0, 0)
    Ay(3)
    Bz(2, 4)
    Aend(1)
    Az(2, 1)
    backward(0)
    By(2)
    Bend(1)
    Az(2, 2)
    Bz(3, 1)
    gathered(1)
    project(1, 1)
    Az(2, 3)
    Bz(3, 2)
    project(1, 0)
    By2(2)
    Az(2, 4)
    Bz(3, 3)
    backward(1)
    Aend(2)
    Az(3, 1)
    Bz(3, 4)
    By(3)
    Bend(2)
    Az(3, 2)
    gathered(2)
    project(2, 1)
    Az(3, 3)
    By2(3)
    project(2, 0)
    Az(3, 4)
    backward(2)
    Aend(3)
    Bend(3)
    gathered(3)
    project(3, 1)
    project(3, 0)
    backward(3)
    collect()
    for h in range(STAGES):
        need(("gnear", h), ("gfar", h))
        lane = slice(h * HEAD, (h + 1) * HEAD)
        for i, ref in enumerate((gk_ref, gv_ref)):
            total = own[i, :, lane] + g_recv[h, 0, i].astype(jnp.float32)
            ref[:, lane] = (total + g_recv[h, 1, i].astype(jnp.float32)).astype(jnp.bfloat16)
    for k in range(4):
        cols = slice(k * 512, (k + 1) * 512)
        need(("out", k))
        out_ref[:, cols] = (acc[0, :, cols] + out_recv[k].astype(jnp.float32)).astype(jnp.bfloat16)
    links.finish()


def local(queries, keys, values, windows, out_weight, grad_out):
    vmem = pl.BlockSpec(memory_space=pltpu.VMEM)
    bf, f32 = jnp.bfloat16, jnp.float32
    n_copies = 200
    return pl.pallas_call(
        kernel,
        out_shape=(
            jax.ShapeDtypeStruct((SLAB, 2048), bf),
            jax.ShapeDtypeStruct((SLAB, 2048), bf),
            jax.ShapeDtypeStruct((SLAB, 512), bf),
            jax.ShapeDtypeStruct((SLAB, 512), bf),
        ),
        in_specs=[vmem, vmem, vmem, pl.BlockSpec(memory_space=pltpu.SMEM), vmem, vmem],
        out_specs=(vmem,) * 4,
        scratch_shapes=[
            pltpu.VMEM((STAGES, NY, NZ, 2, 2, 32, 512), bf),
            pltpu.VMEM((2, 4 * SLAB, 512), bf),
            pltpu.VMEM((SLAB, 2048), bf),
            pltpu.VMEM((SLAB, 4 * SLAB), jnp.int32),
            pltpu.VMEM((16, SLAB, 4 * SLAB), f32),
            pltpu.VMEM((SLAB, 2048), bf),
            pltpu.VMEM((SLAB, 512), f32),
            pltpu.VMEM((2, SLAB, 2048), f32),
            pltpu.VMEM((4, SLAB, 512), bf),
            pltpu.VMEM((4, SLAB, 512), bf),
            pltpu.VMEM((4 * SLAB, 4 * SLAB), bf),
            pltpu.VMEM((4 * SLAB, 4 * SLAB), bf),
            pltpu.VMEM((2, SLAB, 512), f32),
            pltpu.VMEM((STAGES, 2, 2, SLAB, HEAD), bf),
            pltpu.VMEM((STAGES, 2, 2, SLAB, HEAD), bf),
            pltpu.VMEM((16, 512), f32),
            pltpu.VMEM((3, 16, 512), f32),
            pltpu.VMEM((NZ - 1, 16, 512), f32),
            pltpu.VMEM((NY - 1, 16, 512), f32),
            pltpu.SemaphoreType.DMA((n_copies,)),
            pltpu.SemaphoreType.DMA((n_copies,)),
            pltpu.SemaphoreType.DMA((STAGES,)),
            pltpu.SemaphoreType.DMA((15,)),
            pltpu.SemaphoreType.DMA((15,)),
        ],
        compiler_params=pltpu.CompilerParams(
            collective_id=0, has_side_effects=True, vmem_limit_bytes=58 << 20
        ),
    )(queries, keys, values, windows, out_weight.T, grad_out)


def solution(mesh):
    cut = P("seq", "head")
    in_specs = (cut, cut, cut, P("head"), P("head", "seq"), cut)
    return jax.shard_map(
        local, mesh=mesh, in_specs=in_specs, out_specs=(cut,) * 4, check_vma=False
    )
```

time: 919 us -> 144 us (0.16)
  blocking collectives: 837 us -> 0 us
  Pallas kernels: 0 us -> 139 us
  matrix products: 41.5 us -> 0 us
  between operations: 14.1 us -> 0.65 us
    psum x2 -> x0, blocking collectives: 837 us -> none  [the longest x1 549 us: local(): sink_total = lax.psum(sink_part, 'seq')]
    pallas_call x0 -> x1, Pallas kernels: none -> 139 us  [local(): pl.pallas_call(kernel, out_shape=(jax.ShapeDtypeStruct((SLAB, 2048), bf),...]
    dot_general x58 -> x0, matrix products: 41.5 us -> none  [the longest x1 12.5 us: local(): jnp.dot(attn_all, weights_piece, preferred_element_type=jnp.float32)]
  transfers between devices with their start and end apart: 7 -> 0, of which waited for: 0 -> 0; matrix products, arithmetic and copies ran while one was open for 4% -> 0% of each run, Pallas kernels for 0% -> 0%
where the time goes in v1:
time: 144 us
  Pallas kernels  139 us (97%)
  local copies, waits for them, and re-layouts  4.57 us (3%)
    pallas_call x1, Pallas kernels, local(): pl.pallas_call(kernel, out_shape=(jax.ShapeDtypeStruct((SLAB, 2048), bf),...  139 us
    unnamed x10, local copies, waits for them, and re-layouts  4.57 us

profile of v1, /device:TPU:4, one launch (start us, length us, event | category | flops | bytes accessed | tf_op | source)
XLA Modules:
  0.0 143.9 jit_solution(307169719004134266)
XLA Ops:
  0.6 138.7 %shard_map.93 = (bf16[128,2048]{1,0:T(8,128)(2,1)}, bf16[128,2048]{1,0:T(8,128)(2,1)}, bf16[128,512]{1,0:T(8,128)(2,1)}, bf16[128,512]{1,0:T(8,128)(2,1)}) custom-call(bf16[128,2048]{1,0:T(8,128)(2,1)} %q_ref.1, bf16[128,512]{1,0:T(8,128)(2,1)} %k_ref.1, bf16[128,512]{1,0:T(8,128)(2,1)} %v_ref.1, s32[16]{0:T(128)} %win_ref.1, bf16[32,2048]{1,0:T(8,128)(2,1)} %bitcast.1, ...), custom_call_target="tpu_custom_call" | custom-call | tf_op jit(solution)/shard_map/pallas_call | solution.py:486
  139.4 0.0 copy-start
  139.4 1.9 %copy.14 = bf16[128,2048]{1,0:T(8,128)(2,1)} copy(bf16[128,2048]{1,0:T(8,128)(2,1)} %get-tuple-element.8) | data formatting | bytes 1048576
  141.3 0.0 copy-done
  141.3 0.0 copy-start.2
  141.3 0.8 copy.15
  142.1 0.2 copy-done.2
  142.3 0.0 copy-start.1
  142.3 0.7 copy.16
  143.0 0.3 copy-done.1
  143.3 0.7 copy.17
Async XLA Ops:
  139.4 2.0 %copy-start = (bf16[128,2048]{1,0:T(8,128)(2,1)S(1)}, bf16[128,2048]{1,0:T(8,128)(2,1)}, u32[]{:S(2)}) copy-start(bf16[128,2048]{1,0:T(8,128)(2,1)} %get-tuple-element.9) | copy-start | bytes 1572868
  141.3 1.0 copy-start.2
  142.3 1.0 copy-start.1

commit v2 on v1

v2 whole, which is shorter than its diff:
```python
import functools
import math

import jax
import jax.numpy as jnp
from jax import lax
from jax.experimental import pallas as pl
from jax.experimental.pallas import tpu as pltpu
from jax.sharding import PartitionSpec as P

HEAD = 128
SINKS = 4
SLAB = 128
NY, NZ = 4, 8
MASKED = -1e30
FAR_AWAY = 1 << 20
MESH = pl.DeviceIdType.MESH
SCALE = 1.0 / math.sqrt(HEAD)
EXP2_SCALE = SCALE * math.log2(math.e)
Y_FIRST = (256, 128, 128, 512)
STAGES = 4

ORDER = [
    ("x", 0), ("x", 1), ("x", 2), ("x", 3), ("near",), ("far",), ("go", 0), ("go", 1), ("go", 2), ("go", 3),
    ("Ay", 0, 1), ("Ay", 0, -1), ("Ay", 0, 2), ("Bz", 0, 1, 1), ("Bz", 0, 1, -1), ("By", 0, 1, 0),
    ("By", 0, -1, 0), ("Bz", 1, 1, 1), ("Bz", 1, 1, -1), ("Ay", 1, 1), ("Ay", 1, -1), ("Ay", 1, 2),
    ("By", 1, 1, 0), ("By", 1, -1, 0), ("Bz", 2, 1, 1), ("Bz", 2, 1, -1), ("Ay", 2, 1), ("Ay", 2, -1),
    ("Ay", 2, 2), ("S", 1), ("By", 2, 1, 0), ("By", 2, -1, 0), ("Ay", 3, 1), ("Ay", 3, 2), ("Ay", 3, -1),
    ("Bz", 0, 2, 1), ("Bz", 0, 2, -1), ("Bz", 1, 2, 1), ("Bz", 1, 2, -1), ("sA0", 0), ("Az", 0, 1, 1, None),
    ("By", 0, -1, -1), ("Az", 0, 1, -1, None), ("By", 0, -1, 1), ("Bz", 2, 2, 1), ("Bz", 2, 2, -1), ("S", 2),
    ("sA0", 1), ("Az", 1, 1, 1, None), ("Az", 1, 1, -1, None), ("By", 0, 1, 1), ("By", 1, -1, -1),
    ("By", 0, 1, -1), ("Bz", 0, 3, 1), ("Bz", 0, 3, -1), ("By", 0, -1, -2), ("By", 0, 1, 2), ("Bz", 1, 3, 1),
    ("Bz", 1, 3, -1), ("By", 0, -1, 2), ("sA0", 2), ("By", 0, 1, -2), ("By", 1, -1, -2),
    ("Az", 2, 1, 1, None), ("By2", 0, 1, 0), ("Az", 2, 1, -1, None), ("S", 3), ("F", 0), ("sAz", 0, 1, 1),
    ("sAz", 0, 1, -1), ("By2", 0, -1, -1), ("Az", 0, 2, 1, None), ("Az", 0, 2, -1, None), ("By", 1, 1, 1),
    ("By", 1, 1, -1), ("By", 1, -1, 1), ("By", 1, -1, 2), ("sA0", 3), ("F", 1), ("By2", 0, 1, 1),
    ("sAz", 1, 1, 1), ("Bz", 0, 4, 1), ("Bz", 0, 4, -1), ("By", 0, -1, -3), ("By", 0, 1, 3), ("By", 0, 1, -3),
    ("By", 0, -1, 3), ("By2", 0, 1, 2), ("By2", 0, -1, -2), ("sAz", 1, 1, -1), ("Az", 1, 2, 1, None),
    ("Az", 1, 2, -1, None), ("F", 2), ("Bz", 1, 4, 1), ("Bz", 1, 4, -1), ("By", 1, 1, 2), ("By", 1, 1, -2),
    ("By", 1, -1, -3), ("By", 1, -1, 3), ("Bz", 2, 3, 1), ("Bz", 2, 3, -1), ("sAz", 2, 1, 1),
    ("sAz", 2, 1, -1), ("Az", 2, 2, 1, None), ("By", 1, 1, 3), ("By2", 1, -1, -1), ("Az", 2, 2, -1, None),
    ("F", 3), ("By", 1, 1, -3), ("By2", 1, -1, -2), ("sAz", 0, 2, 1), ("sAz", 0, 2, -1), ("By2", 0, 1, 3),
    ("By2", 0, -1, -3), ("Az", 0, 3, 1, None), ("sB0", 0), ("Az", 0, 3, -1, None), ("By", 0, 1, 4),
    ("By", 0, -1, 4), ("By2", 1, 1, 0), ("By", 2, -1, -1), ("sAz", 1, 2, 1), ("sAz", 1, 2, -1),
    ("Az", 1, 3, 1, None), ("Az", 1, 3, -1, None), ("sB0", 1), ("By", 1, 1, 4), ("By", 1, -1, 4),
    ("Bz", 2, 4, 1), ("Bz", 2, 4, -1), ("By2", 1, 1, 1), ("By2", 1, -1, -3), ("Az", 3, 1, 1, 0),
    ("Az", 3, 1, -1, 0), ("sAz", 2, 2, 1), ("By2", 1, 1, 2), ("sAz", 2, 2, -1), ("By", 2, -1, -2),
    ("Az", 2, 3, 1, None), ("Az", 2, 3, -1, None), ("By2", 1, 1, 3), ("By", 2, -1, 1), ("Az", 3, 1, 1, 1),
    ("By", 2, 1, 1), ("By", 2, -1, -3), ("sBy", 0, 1), ("sBy", 0, -1), ("Az", 3, 1, -1, 1), ("sAz", 0, 3, 1),
    ("sAz", 0, 3, -1), ("By", 2, 1, -1), ("By2", 0, -1, 4), ("Az", 0, 4, 1, None), ("Az", 0, 4, -1, None),
    ("By", 2, -1, 2), ("sAz", 1, 3, 1), ("sAz", 1, 3, -1), ("By", 2, 1, 2), ("sBy", 1, 1), ("sBy", 1, -1),
    ("sB0", 2), ("Az", 1, 4, 1, None), ("Az", 1, 4, -1, None), ("By2", 1, -1, 4), ("By", 2, 1, -2),
    ("Az", 3, 1, 1, 2), ("Az", 3, 1, -1, 2), ("By", 2, -1, 4), ("By", 2, 1, 3), ("Az", 3, 1, 1, 3),
    ("Az", 3, 1, -1, 3), ("By", 2, -1, 3), ("By", 2, 1, -3), ("sAz", 2, 3, 1), ("sAz", 2, 3, -1),
    ("By2", 2, -1, -1), ("Az", 2, 4, 1, None), ("By", 2, 1, 4), ("Az", 2, 4, -1, None), ("Az", 3, 2, 1, 0),
    ("Az", 3, 2, -1, 0), ("By2", 2, -1, -2), ("sB2", 0), ("By2", 2, 1, 0), ("By2", 2, -1, -3), ("sA4", 0),
    ("Az", 3, 2, 1, 1), ("By2", 2, 1, 1), ("Az", 3, 2, -1, 1), ("sA4", 1), ("sB2", 1), ("By2", 2, 1, 2),
    ("Az", 3, 2, 1, 2), ("Az", 3, 2, -1, 2), ("By2", 2, -1, 4), ("PJ", 0), ("By2", 2, 1, 3), ("sBy", 2, -1),
    ("sAz", 3, 1, 1), ("sA4", 2), ("sAz", 3, 1, -1), ("Az", 3, 2, 1, 3), ("Az", 3, 2, -1, 3), ("sBy", 2, 1),
    ("BW", 0), ("Az", 3, 3, 1, 0), ("Az", 3, 3, -1, 0), ("PJ", 1), ("Az", 3, 3, 1, 1), ("Az", 3, 3, -1, 1),
    ("BW", 1), ("Az", 3, 3, 1, 2), ("Az", 3, 3, -1, 2), ("sB2", 2), ("sAz", 3, 2, 1), ("sAz", 3, 2, -1),
    ("Az", 3, 3, 1, 3), ("Az", 3, 3, -1, 3), ("Az", 3, 4, 1, 0), ("PJ", 2), ("Az", 3, 4, 1, 1), ("BW", 2),
    ("Az", 3, 4, -1, 2), ("PZ", 3, 0, 1), ("PZ", 3, 1, 1), ("PZ", 3, 1, -1), ("PZ", 3, 2, 1),
    ("sAz", 3, 3, 1), ("sAz", 3, 3, -1), ("Az", 3, 4, -1, 3), ("PZ", 3, 2, -1), ("PZ", 3, 3, 1),
    ("PZ", 3, 3, -1), ("sA4", 3), ("PZ", 3, 4, 1), ("BW", 3),
]


def dot(a, b, ca, cb):
    return lax.dot_general(a, b, (((ca,), (cb,)), ((), ())), preferred_element_type=jnp.float32)


class Links:
    def __init__(self, send_sems, recv_sems):
        self.send_sems, self.recv_sems = send_sems, recv_sems
        self.copies, self.arrived = {}, set()

    def start(self, name, src, dst, device):
        n = len(self.copies)
        copy = pltpu.make_async_remote_copy(
            src_ref=src,
            dst_ref=dst,
            send_sem=self.send_sems.at[n],
            recv_sem=self.recv_sems.at[n],
            device_id=device,
            device_id_type=MESH,
        )
        copy.start()
        self.copies[name] = copy

    def need(self, *names):
        for name in names:
            if name not in self.arrived:
                self.arrived.add(name)
                self.copies[name].wait_recv()

    def finish(self):
        self.need(*self.copies)
        for copy in self.copies.values():
            copy.wait_send()


def kernel(
    q_ref, k_ref, v_ref, win_ref, w_ref, go_ref,
    out_ref, gq_ref, gk_ref, gv_ref,
    G, kv, go_other, dist, probs, attn, ga, acc, out_send, out_recv, ds_buf, pl_buf, own,
    g_send, g_recv, sinks, sink_r1, sink_r2,
    send_sems, recv_sems, local_sems, tree_send, tree_recv,
):
    s, hd = lax.axis_index("seq"), lax.axis_index("head")
    c, x, z, y = s % 2, (s // 2) % 2, (s // 4) % NZ, s // (4 * NZ)
    n_seq = 4 * NY * NZ

    def at(y, z, x, c):
        return (((y * NZ + z) * 2 + x) * 2 + c, hd)

    def ym(k):
        return (y + k + NY) % NY

    def zm(k):
        return (z + k + NZ) % NZ

    y_dev = {k: at(ym(k), z, x, c) for k in (1, -1, 2)}
    z_dev = {k: at(y, zm(k), x, c) for k in (1, -1)}
    x_dev, sib, pair = at(y, z, 1 - x, c), at(y, z, x, 1 - c), (s, 1 - hd)
    after1, after2 = ((s + 1) % n_seq, hd), ((s + 2) % n_seq, hd)
    before1, before2 = ((s + n_seq - 1) % n_seq, hd), ((s + n_seq - 2) % n_seq, hd)
    quad = 2 * x + c
    leader = quad == 0
    column_leader = leader & (z == 0)
    place = y * NZ + z
    root = column_leader & (y == 0)

    barrier = pltpu.get_barrier_semaphore()

    def hello(device):
        pl.semaphore_signal(barrier, inc=1, device_id=device, device_id_type=MESH)

    everyone = [y_dev[1], y_dev[-1], y_dev[2], z_dev[1], z_dev[-1], x_dev, sib, pair,
                after1, after2, before1, before2]
    for device in everyone:
        hello(device)

    @pl.when(leader)
    def _():
        for k in range(1, 4):
            hello(at(y, z, k // 2, k % 2))

    @pl.when(column_leader)
    def _():
        for k in range(1, NZ):
            hello(at(y, k, 0, 0))

    @pl.when(root)
    def _():
        for k in range(1, NY * NZ):
            hello(at(k // NZ, k % NZ, 0, 0))

    @pl.when(quad != 0)
    def _():
        hello(at(y, z, 0, 0))

    @pl.when(leader & (z != 0))
    def _():
        hello(at(y, 0, 0, 0))

    @pl.when(leader & (place != 0))
    def _():
        hello(at(0, 0, 0, 0))

    leader_peers = 3 + jnp.where(z != 0, 1, NZ - 1) + jnp.where(place != 0, 1, NY * NZ - 1)
    pl.semaphore_wait(barrier, len(everyone) + jnp.where(quad != 0, 1, leader_peers))

    links = Links(send_sems, recv_sems)
    start, need = links.start, links.need

    locals_ = []
    for h in range(STAGES):
        piece = w_ref.at[:, pl.ds(h * 512, 512)]
        mine = G.at[h, y, z, x, c]
        copy = pltpu.make_async_copy(piece, mine, local_sems.at[h])
        copy.start()
        locals_.append(copy)

    kv[0, 2 * SLAB : 3 * SLAB, :] = k_ref[...]
    kv[1, 2 * SLAB : 3 * SLAB, :] = v_ref[...]
    kv[:, 3 * SLAB + 16 :, :] = jnp.zeros((2, SLAB - 16, 512), jnp.bfloat16)
    own_kv = kv.at[:, pl.ds(2 * SLAB, SLAB)]
    first16 = kv.at[:, pl.ds(2 * SLAB, 16)]
    sink_kv = kv.at[:, pl.ds(3 * SLAB, 16)]

    def tree_copy(src, slot, rslot, device):
        return pltpu.make_async_remote_copy(
            src_ref=src, dst_ref=sink_kv, send_sem=tree_send.at[slot], recv_sem=tree_recv.at[rslot],
            device_id=device, device_id_type=MESH)

    def spread(level):
        if level == 0:

            @pl.when(root)
            def _():
                kv[:, 3 * SLAB : 3 * SLAB + 16, :] = kv[:, 2 * SLAB : 2 * SLAB + 16, :]
                for k in range(1, NY):
                    tree_copy(first16, k, 0, at(k, 0, 0, 0)).start()

        if level == 1:

            @pl.when(column_leader & (y != 0))
            def _():
                tree_copy(first16, 0, 0, sib).wait_recv()

            @pl.when(column_leader)
            def _():
                for k in range(1, NZ):
                    tree_copy(sink_kv, 3 + k, 0, at(y, k, 0, 0)).start()

        if level == 2:

            @pl.when(leader & (z != 0))
            def _():
                tree_copy(first16, 0, 0, sib).wait_recv()

            @pl.when(leader)
            def _():
                for k in range(1, 4):
                    tree_copy(sink_kv, 10 + k, 0, at(y, z, k // 2, k % 2)).start()

        if level == 3:

            @pl.when(quad != 0)
            def _():
                tree_copy(first16, 0, 0, sib).wait_recv()

            @pl.when(leader)
            def _():
                for k in range(1, 4):
                    tree_copy(sink_kv, 10 + k, 0, at(y, z, k // 2, k % 2)).wait_send()

            @pl.when(column_leader)
            def _():
                for k in range(1, NZ):
                    tree_copy(sink_kv, 3 + k, 0, at(y, k, 0, 0)).wait_send()

            @pl.when(root)
            def _():
                for k in range(1, NY):
                    tree_copy(first16, k, 0, at(k, 0, 0, 0)).wait_send()

    def lanes(h, first):
        return pl.ds(0, Y_FIRST[h]) if first else pl.ds(Y_FIRST[h], 512 - Y_FIRST[h])

    def block(h, first, ys, zs, xs=pl.ds(0, 2)):
        return G.at[h, ys, zs, xs, c, :, lanes(h, first)]

    one = lambda i: pl.ds(i, 1)
    all_y, all_z = pl.ds(0, NY), pl.ds(0, NZ)
    both = (1, -1)
    ready = set()

    def push(name, ref, device):
        start(name, ref, ref, device)

    def have_x(h):
        if h not in ready:
            ready.add(h)
            locals_[h].wait()
        need(("x", h))

    def halves(h):
        return range(NY) if Y_FIRST[h] == 512 else (None,)

    def last_z(h):
        names = []
        for q in halves(h):
            for d in both:
                if q is None or (q < 2) == (d == 1):
                    names.append(("Az", h, 4, d, q))
        return names

    plus = (0, 1, 2, 3)

    def near():
        start("near", own_kv, kv.at[:, pl.ds(SLAB, SLAB)], after1)

    def far():
        start("far", own_kv, kv.at[:, pl.ds(0, SLAB)], after2)

    def go(i):
        piece = pl.ds(i * 512, 512)
        start(("go", i), go_ref.at[:, piece], go_other.at[:, piece], pair)

    def x_(h):
        start(("x", h), w_ref.at[:, pl.ds(h * 512, 512)], G.at[h, y, z, x, c], x_dev)

    def Ay(h, k):
        have_x(h)
        push(("Ay", h, k), block(h, True, one(y), one(z)), y_dev[k])

    def Az(h, k, d, q):
        if k == 1:
            need(*[("Ay", h, j) for j in (1, -1, 2)])
        else:
            need(("Az", h, k - 1, d, q))
        ys = all_y if q is None else one(q)
        if k == 4 and q is None:
            ys = pl.ds(0 if d == 1 else 2, 2)
        push(("Az", h, k, d, q), block(h, True, ys, one(zm(-d * (k - 1)))), z_dev[d])

    def sA0(h):
        need(*[("Ay", h, j) for j in (1, -1, 2)])
        push(("sA0", h), block(h, True, all_y, one(z)), sib)

    def sAz(h, k, d):
        need(*[("Az", h, k, d, q) for q in halves(h)])
        push(("sAz", h, k, d), block(h, True, all_y, one(zm(-d * k))), sib)

    def sA4(h):
        need(*last_z(h))
        push(("sA4", h), block(h, True, all_y, one(zm(4))), sib)

    def Bz(h, k, d):
        if k == 1:
            have_x(h)
        else:
            need(("Bz", h, k - 1, d))
        xs = pl.ds(0, 2) if k < 4 else one(0 if d == 1 else 1)
        push(("Bz", h, k, d), block(h, False, one(y), one(zm(-d * (k - 1))), xs), z_dev[d])

    def have_z(h, r):
        if r == 0:
            have_x(h)
        elif r == 4:
            need(("Bz", h, 4, 1), ("Bz", h, 4, -1))
        else:
            need(("Bz", h, abs(r), -1 if r > 0 else 1))

    def By(h, d, r):
        have_z(h, r)
        push(("By", h, d, r), block(h, False, one(y), one(zm(r))), y_dev[d])

    def By2(h, d, r):
        need(("By", h, d, r))
        push(("By2", h, d, r), block(h, False, one(ym(-d)), one(zm(r))), y_dev[d])

    def sB0(h):
        for r in range(-3, 5):
            have_z(h, r)
        push(("sB0", h), block(h, False, one(y), all_z), sib)

    def sBy(h, d):
        need(*[("By", h, d, r) for r in range(-3, 5)])
        push(("sBy", h, d), block(h, False, one(ym(-d)), all_z), sib)

    def sB2(h):
        need(*[("By2", h, 1 if r in plus else -1, r) for r in range(-3, 5)])
        push(("sB2", h), block(h, False, one(ym(2)), all_z), sib)

    def gathered(h):
        names = [("sA0", h), ("sA4", h), ("sB0", h), ("sB2", h), ("sBy", h, 1), ("sBy", h, -1)]
        need(*names, *[("sAz", h, k, d) for k in (1, 2, 3) for d in both])

    def masks():
        row = lax.broadcasted_iota(jnp.int32, (SLAB, 4 * SLAB), 0)
        col = lax.broadcasted_iota(jnp.int32, (SLAB, 4 * SLAB), 1)
        first = s * SLAB
        gap = row - col + 2 * SLAB
        band = (col < 3 * SLAB) & (gap >= 0) & (first - 2 * SLAB + col >= SINKS)
        place = col - 3 * SLAB
        sink = (place >= 0) & (place < SINKS) & (place <= first + row)
        dist[...] = jnp.where(band, gap, jnp.where(sink, 0, FAR_AWAY))

    def forward(h):
        need("near", "far")
        keys, vals = kv[0, :, h * HEAD : (h + 1) * HEAD], kv[1, :, h * HEAD : (h + 1) * HEAD]
        for j in range(4 * h, 4 * h + 4):
            cols = slice(j * HEAD, (j + 1) * HEAD)
            scores = dot(q_ref[:, cols], keys, 1, 1)
            scores = jnp.where(dist[...] < win_ref[j], scores, MASKED)
            top = jnp.max(scores, axis=1, keepdims=True)
            p = jnp.exp2((scores - top) * EXP2_SCALE)
            p = p * (1.0 / jnp.sum(p, axis=1, keepdims=True))
            probs[j] = p
            attn[:, cols] = dot(p.astype(jnp.bfloat16), vals, 1, 0).astype(jnp.bfloat16)

    def project(h):
        gathered(h)
        need(*[("go", i) for i in range(4)])
        rows = slice(h * 512, (h + 1) * 512)
        for half in range(2):
            for k in range(4):
                yy, z0 = k // 2, (k % 2) * 4
                w = G[h, 2 * (hd if half == 0 else 1 - hd) + yy, z0 : z0 + 4].reshape(512, 512)
                o = dot(attn[:, rows], w, 1, 1)
                for i in range(4):
                    part = o[:, i * 128 : (i + 1) * 128]
                    acc[half, yy, z0 + i] = part if h == 0 else acc[half, yy, z0 + i] + part
                cols = slice(k * 512, (k + 1) * 512)
                g = dot((go_ref if half == 0 else go_other)[:, cols], w, 1, 0)
                ga[...] = g if half == 0 and k == 0 else ga[...] + g

    def out_lanes(yy, zz):
        return pl.ds(pl.multiple_of(yy * 1024 + zz * 128, 128), 128)

    def project_z(h, k, d):
        if k == 0:
            need(("sA0", h), *[("Ay", h, j) for j in (1, -1, 2)])
        elif k == 4:
            need(("sA4", h), *last_z(h))
        else:
            need(("sAz", h, k, d), *[("Az", h, k, d, q) for q in halves(h)])
        rows = slice(h * 512, (h + 1) * 512)
        zz, n = zm(-d * k), len(sent)
        sent.append(zz)
        for half in (1, 0):
            w = G[h, pl.ds(2 * (hd if half == 0 else 1 - hd), 2), zz].reshape(256, 512)
            o = dot(attn[:, rows], w, 1, 1)
            for yy in range(2):
                part = acc[half, yy, zz] + o[:, yy * 128 : (yy + 1) * 128]
                if half == 1:
                    out_send[n, yy] = part.astype(jnp.bfloat16)
                else:
                    acc[half, yy, zz] = part
            if half == 1:
                start(("out", n), out_send.at[n], out_recv.at[n], pair)
            side = go_ref if half == 0 else go_other
            cols = jnp.concatenate([side[:, out_lanes(0, zz)], side[:, out_lanes(1, zz)]], axis=1)
            g = dot(cols, w, 1, 0)
            ga[...] = g if n == 0 and half == 1 else ga[...] + g

    def backward(h):
        keys, vals = kv[0, :, h * HEAD : (h + 1) * HEAD], kv[1, :, h * HEAD : (h + 1) * HEAD]
        for i in range(4):
            j = 4 * h + i
            cols = slice(j * HEAD, (j + 1) * HEAD)
            g = ga[:, i * HEAD : (i + 1) * HEAD].astype(jnp.bfloat16)
            delta = jnp.sum(
                g.astype(jnp.float32) * attn[:, cols].astype(jnp.float32), axis=1, keepdims=True
            )
            p = probs[j]
            ds = (p * (dot(g, vals, 1, 1) - delta) * SCALE).astype(jnp.bfloat16)
            gq_ref[:, cols] = dot(ds, keys, 1, 0).astype(jnp.bfloat16)
            ds_buf[i * SLAB : (i + 1) * SLAB, :] = ds
            pl_buf[i * SLAB : (i + 1) * SLAB, :] = p.astype(jnp.bfloat16)
        g4 = jnp.concatenate([ga[:, i * HEAD : (i + 1) * HEAD] for i in range(4)], axis=0)
        q4 = jnp.concatenate(
            [q_ref[:, (4 * h + i) * HEAD : (4 * h + i + 1) * HEAD] for i in range(4)], axis=0
        )
        lane = slice(h * HEAD, (h + 1) * HEAD)
        dk = dot(ds_buf[...], q4, 0, 0)
        dv = dot(pl_buf[...], g4.astype(jnp.bfloat16), 0, 0)
        for i, d in enumerate((dk, dv)):
            g_send[h, 0, i] = d[:SLAB].astype(jnp.bfloat16)
            g_send[h, 1, i] = d[SLAB : 2 * SLAB].astype(jnp.bfloat16)
            own[i, :, lane] = d[2 * SLAB : 3 * SLAB]
        upper = lax.broadcasted_iota(jnp.int32, (8, HEAD), 0) < SINKS
        sinks[:, lane] = jnp.where(
            upper, dk[3 * SLAB : 3 * SLAB + 8], pltpu.roll(dv[3 * SLAB : 3 * SLAB + 8], SINKS, 0)
        )
        start(("gfar", h), g_send.at[h, 0], g_recv.at[h, 0], before2)
        start(("gnear", h), g_send.at[h, 1], g_recv.at[h, 1], before1)

    def up(dst, slot, device):
        return pltpu.make_async_remote_copy(
            src_ref=sinks, dst_ref=dst, send_sem=tree_send.at[14], recv_sem=tree_recv.at[1 + slot],
            device_id=device, device_id_type=MESH)

    def collect():
        @pl.when(quad != 0)
        def _():
            copy = up(sink_r1.at[quad - 1], quad - 1, at(y, z, 0, 0))
            copy.start()
            copy.wait_send()

        @pl.when(leader)
        def _():
            for k in range(3):
                up(sink_r1.at[k], k, sib).wait_recv()
            sinks[...] = sinks[...] + sink_r1[0] + sink_r1[1] + sink_r1[2]

            @pl.when(place != 0)
            def _():
                copy = up(sink_r2.at[place - 1], 2 + place, at(0, 0, 0, 0))
                copy.start()
                copy.wait_send()

            @pl.when(place == 0)
            def _():
                total = sinks[...]
                for k in range(NY * NZ - 1):
                    up(sink_r2.at[k], 3 + k, sib).wait_recv()
                    total = total + sink_r2[k]
                keep = lax.broadcasted_iota(jnp.int32, (8, 512), 0) < SINKS
                own[0, 0:8, :] = own[0, 0:8, :] + jnp.where(keep, total, 0.0)
                own[1, 0:8, :] = own[1, 0:8, :] + jnp.where(keep, pltpu.roll(total, SINKS, 0), 0.0)

    sent = []
    act = dict(x=x_, near=near, far=far, go=go, Ay=Ay, Az=Az, sA0=sA0, sAz=sAz, sA4=sA4, Bz=Bz, By=By,
               By2=By2, sB0=sB0, sBy=sBy, sB2=sB2, S=spread, F=forward, PJ=project, PZ=project_z, BW=backward)
    spread(0)
    masks()
    for name, *where in ORDER:
        act[name](*where)
    collect()
    for h in range(STAGES):
        need(("gnear", h), ("gfar", h))
        lane = slice(h * HEAD, (h + 1) * HEAD)
        for i, ref in enumerate((gk_ref, gv_ref)):
            total = own[i, :, lane] + g_recv[h, 0, i].astype(jnp.float32)
            ref[:, lane] = (total + g_recv[h, 1, i].astype(jnp.float32)).astype(jnp.bfloat16)
    for n, zz in enumerate(sent):
        need(("out", n))
        for yy in range(2):
            total = acc[0, yy, zz] + out_recv[n, yy].astype(jnp.float32)
            out_ref[:, out_lanes(yy, zz)] = total.astype(jnp.bfloat16)
    links.finish()


def local(queries, keys, values, windows, out_weight, grad_out):
    vmem = pl.BlockSpec(memory_space=pltpu.VMEM)
    bf, f32 = jnp.bfloat16, jnp.float32
    n_copies = 256
    return pl.pallas_call(
        kernel,
        out_shape=(
            jax.ShapeDtypeStruct((SLAB, 2048), bf),
            jax.ShapeDtypeStruct((SLAB, 2048), bf),
            jax.ShapeDtypeStruct((SLAB, 512), bf),
            jax.ShapeDtypeStruct((SLAB, 512), bf),
        ),
        in_specs=[vmem, vmem, vmem, pl.BlockSpec(memory_space=pltpu.SMEM), vmem, vmem],
        out_specs=(vmem,) * 4,
        scratch_shapes=[
            pltpu.VMEM((STAGES, NY, NZ, 2, 2, 32, 512), bf),
            pltpu.VMEM((2, 4 * SLAB, 512), bf),
            pltpu.VMEM((SLAB, 2048), bf),
            pltpu.VMEM((SLAB, 4 * SLAB), jnp.int32),
            pltpu.VMEM((16, SLAB, 4 * SLAB), f32),
            pltpu.VMEM((SLAB, 2048), bf),
            pltpu.VMEM((SLAB, 512), f32),
            pltpu.VMEM((2, 2, NZ, SLAB, HEAD), f32),
            pltpu.VMEM((NZ, 2, SLAB, HEAD), bf),
            pltpu.VMEM((NZ, 2, SLAB, HEAD), bf),
            pltpu.VMEM((4 * SLAB, 4 * SLAB), bf),
            pltpu.VMEM((4 * SLAB, 4 * SLAB), bf),
            pltpu.VMEM((2, SLAB, 512), f32),
            pltpu.VMEM((STAGES, 2, 2, SLAB, HEAD), bf),
            pltpu.VMEM((STAGES, 2, 2, SLAB, HEAD), bf),
            pltpu.VMEM((8, 512), f32),
            pltpu.VMEM((3, 8, 512), f32),
            pltpu.VMEM((NY * NZ - 1, 8, 512), f32),
            pltpu.SemaphoreType.DMA((n_copies,)),
            pltpu.SemaphoreType.DMA((n_copies,)),
            pltpu.SemaphoreType.DMA((STAGES,)),
            pltpu.SemaphoreType.DMA((15,)),
            pltpu.SemaphoreType.DMA((3 + NY * NZ,)),
        ],
        compiler_params=pltpu.CompilerParams(
            collective_id=0, has_side_effects=True, vmem_limit_bytes=58 << 20
        ),
    )(queries, keys, values, windows, out_weight.T, grad_out)


def solution(mesh):
    cut = P("seq", "head")
    in_specs = (cut, cut, cut, P("head"), P("head", "seq"), cut)
    return jax.shard_map(
        local, mesh=mesh, in_specs=in_specs, out_specs=(cut,) * 4, check_vma=False
    )
```

time: 144 us -> 106 us (0.74)
  Pallas kernels: 139 us -> 101 us
    pallas_call x1, Pallas kernels: 139 us -> 101 us  [local(): pl.pallas_call(kernel, out_shape=(jax.ShapeDtypeStruct((SLAB, 2048), bf),...]
where the time goes in v2:
time: 106 us
  Pallas kernels  101 us (95%)
  local copies, waits for them, and re-layouts  4.57 us (4%)
    pallas_call x1, Pallas kernels, local(): pl.pallas_call(kernel, out_shape=(jax.ShapeDtypeStruct((SLAB, 2048), bf),...  101 us
    unnamed x10, local copies, waits for them, and re-layouts  4.57 us

profile of v2, /device:TPU:4, one launch (start us, length us, event | category | flops | bytes accessed | tf_op | source)
XLA Modules:
  0.0 106.1 jit_solution(6275108820408792494)
XLA Ops:
  0.6 100.9 %shard_map.93 = (bf16[128,2048]{1,0:T(8,128)(2,1)}, bf16[128,2048]{1,0:T(8,128)(2,1)}, bf16[128,512]{1,0:T(8,128)(2,1)}, bf16[128,512]{1,0:T(8,128)(2,1)}) custom-call(bf16[128,2048]{1,0:T(8,128)(2,1)} %q_ref.1, bf16[128,512]{1,0:T(8,128)(2,1)} %k_ref.1, bf16[128,512]{1,0:T(8,128)(2,1)} %v_ref.1, s32[16]{0:T(128)} %win_ref.1, bf16[32,2048]{1,0:T(8,128)(2,1)} %bitcast.1, ...), custom_call_target="tpu_custom_call" | custom-call | tf_op jit(solution)/shard_map/pallas_call | solution.py:522
  101.5 0.0 copy-start
  101.5 1.9 %copy.14 = bf16[128,2048]{1,0:T(8,128)(2,1)} copy(bf16[128,2048]{1,0:T(8,128)(2,1)} %get-tuple-element.8) | data formatting | bytes 1048576
  103.5 0.0 copy-done
  103.5 0.0 copy-start.2
  103.5 0.8 copy.15
  104.3 0.2 copy-done.2
  104.5 0.0 copy-start.1
  104.5 0.7 copy.16
  105.1 0.3 copy-done.1
  105.4 0.7 copy.17
Async XLA Ops:
  101.5 2.0 %copy-start = (bf16[128,2048]{1,0:T(8,128)(2,1)S(1)}, bf16[128,2048]{1,0:T(8,128)(2,1)}, u32[]{:S(2)}) copy-start(bf16[128,2048]{1,0:T(8,128)(2,1)} %get-tuple-element.9) | copy-start | bytes 1572868
  103.5 1.0 copy-start.2
  104.5 1.0 copy-start.1

commit v3 on v2

--- a/solution.py
+++ b/solution.py
@@ -17,52 +17,57 @@
 MESH = pl.DeviceIdType.MESH
 SCALE = 1.0 / math.sqrt(HEAD)
 EXP2_SCALE = SCALE * math.log2(math.e)
-Y_FIRST = (256, 128, 128, 512)
+Y_FIRST = (128, 128, 128, 512)
 STAGES = 4
 
 ORDER = [
-    ("x", 0), ("x", 1), ("x", 2), ("x", 3), ("near",), ("far",), ("go", 0), ("go", 1), ("go", 2), ("go", 3),
-    ("Ay", 0, 1), ("Ay", 0, -1), ("Ay", 0, 2), ("Bz", 0, 1, 1), ("Bz", 0, 1, -1), ("By", 0, 1, 0),
-    ("By", 0, -1, 0), ("Bz", 1, 1, 1), ("Bz", 1, 1, -1), ("Ay", 1, 1), ("Ay", 1, -1), ("Ay", 1, 2),
-    ("By", 1, 1, 0), ("By", 1, -1, 0), ("Bz", 2, 1, 1), ("Bz", 2, 1, -1), ("Ay", 2, 1), ("Ay", 2, -1),
-    ("Ay", 2, 2), ("S", 1), ("By", 2, 1, 0), ("By", 2, -1, 0), ("Ay", 3, 1), ("Ay", 3, 2), ("Ay", 3, -1),
-    ("Bz", 0, 2, 1), ("Bz", 0, 2, -1), ("Bz", 1, 2, 1), ("Bz", 1, 2, -1), ("sA0", 0), ("Az", 0, 1, 1, None),
-    ("By", 0, -1, -1), ("Az", 0, 1, -1, None), ("By", 0, -1, 1), ("Bz", 2, 2, 1), ("Bz", 2, 2, -1), ("S", 2),
-    ("sA0", 1), ("Az", 1, 1, 1, None), ("Az", 1, 1, -1, None), ("By", 0, 1, 1), ("By", 1, -1, -1),
-    ("By", 0, 1, -1), ("Bz", 0, 3, 1), ("Bz", 0, 3, -1), ("By", 0, -1, -2), ("By", 0, 1, 2), ("Bz", 1, 3, 1),
-    ("Bz", 1, 3, -1), ("By", 0, -1, 2), ("sA0", 2), ("By", 0, 1, -2), ("By", 1, -1, -2),
-    ("Az", 2, 1, 1, None), ("By2", 0, 1, 0), ("Az", 2, 1, -1, None), ("S", 3), ("F", 0), ("sAz", 0, 1, 1),
-    ("sAz", 0, 1, -1), ("By2", 0, -1, -1), ("Az", 0, 2, 1, None), ("Az", 0, 2, -1, None), ("By", 1, 1, 1),
-    ("By", 1, 1, -1), ("By", 1, -1, 1), ("By", 1, -1, 2), ("sA0", 3), ("F", 1), ("By2", 0, 1, 1),
-    ("sAz", 1, 1, 1), ("Bz", 0, 4, 1), ("Bz", 0, 4, -1), ("By", 0, -1, -3), ("By", 0, 1, 3), ("By", 0, 1, -3),
-    ("By", 0, -1, 3), ("By2", 0, 1, 2), ("By2", 0, -1, -2), ("sAz", 1, 1, -1), ("Az", 1, 2, 1, None),
-    ("Az", 1, 2, -1, None), ("F", 2), ("Bz", 1, 4, 1), ("Bz", 1, 4, -1), ("By", 1, 1, 2), ("By", 1, 1, -2),
-    ("By", 1, -1, -3), ("By", 1, -1, 3), ("Bz", 2, 3, 1), ("Bz", 2, 3, -1), ("sAz", 2, 1, 1),
-    ("sAz", 2, 1, -1), ("Az", 2, 2, 1, None), ("By", 1, 1, 3), ("By2", 1, -1, -1), ("Az", 2, 2, -1, None),
-    ("F", 3), ("By", 1, 1, -3), ("By2", 1, -1, -2), ("sAz", 0, 2, 1), ("sAz", 0, 2, -1), ("By2", 0, 1, 3),
-    ("By2", 0, -1, -3), ("Az", 0, 3, 1, None), ("sB0", 0), ("Az", 0, 3, -1, None), ("By", 0, 1, 4),
-    ("By", 0, -1, 4), ("By2", 1, 1, 0), ("By", 2, -1, -1), ("sAz", 1, 2, 1), ("sAz", 1, 2, -1),
-    ("Az", 1, 3, 1, None), ("Az", 1, 3, -1, None), ("sB0", 1), ("By", 1, 1, 4), ("By", 1, -1, 4),
-    ("Bz", 2, 4, 1), ("Bz", 2, 4, -1), ("By2", 1, 1, 1), ("By2", 1, -1, -3), ("Az", 3, 1, 1, 0),
-    ("Az", 3, 1, -1, 0), ("sAz", 2, 2, 1), ("By2", 1, 1, 2), ("sAz", 2, 2, -1), ("By", 2, -1, -2),
-    ("Az", 2, 3, 1, None), ("Az", 2, 3, -1, None), ("By2", 1, 1, 3), ("By", 2, -1, 1), ("Az", 3, 1, 1, 1),
-    ("By", 2, 1, 1), ("By", 2, -1, -3), ("sBy", 0, 1), ("sBy", 0, -1), ("Az", 3, 1, -1, 1), ("sAz", 0, 3, 1),
-    ("sAz", 0, 3, -1), ("By", 2, 1, -1), ("By2", 0, -1, 4), ("Az", 0, 4, 1, None), ("Az", 0, 4, -1, None),
-    ("By", 2, -1, 2), ("sAz", 1, 3, 1), ("sAz", 1, 3, -1), ("By", 2, 1, 2), ("sBy", 1, 1), ("sBy", 1, -1),
-    ("sB0", 2), ("Az", 1, 4, 1, None), ("Az", 1, 4, -1, None), ("By2", 1, -1, 4), ("By", 2, 1, -2),
-    ("Az", 3, 1, 1, 2), ("Az", 3, 1, -1, 2), ("By", 2, -1, 4), ("By", 2, 1, 3), ("Az", 3, 1, 1, 3),
-    ("Az", 3, 1, -1, 3), ("By", 2, -1, 3), ("By", 2, 1, -3), ("sAz", 2, 3, 1), ("sAz", 2, 3, -1),
-    ("By2", 2, -1, -1), ("Az", 2, 4, 1, None), ("By", 2, 1, 4), ("Az", 2, 4, -1, None), ("Az", 3, 2, 1, 0),
-    ("Az", 3, 2, -1, 0), ("By2", 2, -1, -2), ("sB2", 0), ("By2", 2, 1, 0), ("By2", 2, -1, -3), ("sA4", 0),
-    ("Az", 3, 2, 1, 1), ("By2", 2, 1, 1), ("Az", 3, 2, -1, 1), ("sA4", 1), ("sB2", 1), ("By2", 2, 1, 2),
-    ("Az", 3, 2, 1, 2), ("Az", 3, 2, -1, 2), ("By2", 2, -1, 4), ("PJ", 0), ("By2", 2, 1, 3), ("sBy", 2, -1),
-    ("sAz", 3, 1, 1), ("sA4", 2), ("sAz", 3, 1, -1), ("Az", 3, 2, 1, 3), ("Az", 3, 2, -1, 3), ("sBy", 2, 1),
-    ("BW", 0), ("Az", 3, 3, 1, 0), ("Az", 3, 3, -1, 0), ("PJ", 1), ("Az", 3, 3, 1, 1), ("Az", 3, 3, -1, 1),
-    ("BW", 1), ("Az", 3, 3, 1, 2), ("Az", 3, 3, -1, 2), ("sB2", 2), ("sAz", 3, 2, 1), ("sAz", 3, 2, -1),
-    ("Az", 3, 3, 1, 3), ("Az", 3, 3, -1, 3), ("Az", 3, 4, 1, 0), ("PJ", 2), ("Az", 3, 4, 1, 1), ("BW", 2),
-    ("Az", 3, 4, -1, 2), ("PZ", 3, 0, 1), ("PZ", 3, 1, 1), ("PZ", 3, 1, -1), ("PZ", 3, 2, 1),
-    ("sAz", 3, 3, 1), ("sAz", 3, 3, -1), ("Az", 3, 4, -1, 3), ("PZ", 3, 2, -1), ("PZ", 3, 3, 1),
-    ("PZ", 3, 3, -1), ("sA4", 3), ("PZ", 3, 4, 1), ("BW", 3),
+    ("x", 0), ("x", 1), ("x", 2), ("x", 3), ("Ay", 0, 1), ("Ay", 0, -1), ("Ay", 0, 2), ("Bz", 0, 1, 1),
+    ("Bz", 0, 1, -1), ("By", 0, 1, 0), ("By", 0, -1, 0), ("Ay", 1, 1), ("Ay", 1, -1), ("Ay", 1, 2),
+    ("By", 1, 1, 0), ("By", 1, -1, 0), ("Bz", 1, 1, 1), ("Bz", 1, 1, -1), ("Ay", 2, 1), ("Ay", 2, -1),
+    ("Ay", 2, 2), ("By", 2, 1, 0), ("By", 2, -1, 0), ("Bz", 2, 1, 1), ("Bz", 2, 1, -1), ("near",), ("far",),
+    ("Ay", 3, 1), ("Ay", 3, -1), ("Ay", 3, 2), ("sA0", 0), ("Az", 0, 1, -1, None), ("Bz", 0, 2, -1),
+    ("By", 0, -1, -1), ("Bz", 1, 2, -1), ("sA0", 1), ("Az", 1, 1, -1, None), ("By", 0, -1, 1),
+    ("Bz", 2, 2, -1), ("Bz", 0, 2, 1), ("By", 1, -1, -1), ("By2", 0, 1, 0), ("By", 0, 1, 1), ("S", 1),
+    ("far2",), ("Az", 0, 1, 1, None), ("sA0", 2), ("By", 1, -1, 1), ("sAz", 0, 1, -1), ("Az", 0, 2, -1, None),
+    ("By", 0, 1, -1), ("Az", 2, 1, -1, None), ("By", 2, -1, -1), ("Bz", 1, 2, 1), ("By", 0, 1, 2),
+    ("Bz", 0, 3, -1), ("By", 0, -1, 2), ("Az", 1, 1, 1, None), ("go", 0), ("go", 1), ("go", 2),
+    ("By2", 1, 1, 0), ("go", 3), ("Bz", 1, 3, -1), ("By", 1, 1, 1), ("By", 1, -1, 2), ("sAz", 1, 1, -1),
+    ("Az", 2, 1, 1, None), ("Az", 1, 2, -1, None), ("By2", 0, -1, -1), ("S", 2), ("By", 1, 1, -1), ("sA0", 3),
+    ("By", 2, -1, 1), ("Bx", 0, 1, 0), ("Bz", 2, 2, 1), ("By", 1, 1, 2), ("Bz", 2, 3, -1), ("By", 0, -1, -2),
+    ("sAz", 0, 2, -1), ("Bz", 0, 3, 1), ("By2", 0, 1, 1), ("Az", 0, 3, -1, None), ("sAz", 0, 1, 1),
+    ("By2", 1, -1, -1), ("By", 0, 1, -2), ("Az", 0, 2, 1, None), ("By", 2, -1, 2), ("sAz", 2, 1, -1),
+    ("By", 1, 1, -2), ("Az", 2, 2, -1, None), ("By", 1, -1, -2), ("Bz", 1, 3, 1), ("Bx", 1, 1, 0),
+    ("By2", 0, 1, 2), ("sAz", 1, 1, 1), ("Bz", 0, 4, -1), ("By", 0, 1, 3), ("By", 0, -1, 3),
+    ("Az", 1, 2, 1, None), ("S", 3), ("F", 0), ("Bx", 0, -1, -1), ("By2", 1, 1, 1), ("sAz", 1, 2, -1),
+    ("By", 1, 1, 3), ("By", 1, -1, 3), ("Bz", 1, 4, -1), ("Az", 1, 3, -1, None), ("By2", 2, -1, -1),
+    ("sAz", 2, 1, 1), ("Az", 2, 2, 1, None), ("Bz", 2, 4, -1), ("By2", 1, 1, 2), ("By", 2, -1, -2),
+    ("Bx", 0, 1, 1), ("Az", 3, 1, -1, 0), ("Bz", 2, 3, 1), ("F", 1), ("By2", 0, -1, -2), ("sAz", 0, 2, 1),
+    ("sAz", 0, 3, -1), ("Bz", 0, 4, 1), ("By", 0, -1, -3), ("By", 0, 1, -3), ("Az", 0, 3, 1, None),
+    ("Az", 0, 4, -1, None), ("Bx", 1, -1, -1), ("By2", 2, 1, 0), ("Bx", 0, 1, 2), ("By2", 1, -1, -2),
+    ("By", 1, 1, -3), ("sAz", 2, 2, -1), ("By", 1, -1, -3), ("By", 2, 1, 1), ("Bz", 1, 4, 1),
+    ("Az", 2, 3, -1, None), ("F", 2), ("By2", 0, 1, 3), ("Bx", 1, 1, 1), ("sAz", 1, 2, 1), ("sAz", 1, 3, -1),
+    ("Az", 1, 3, 1, None), ("Az", 1, 4, -1, None), ("By2", 1, 1, 3), ("Bx", 2, -1, -1), ("By", 2, 1, -1),
+    ("By", 2, -1, 3), ("sAz", 2, 2, 1), ("Az", 2, 3, 1, None), ("Bx", 1, 1, 2), ("Az", 3, 1, -1, 1),
+    ("Az", 3, 1, -1, 2), ("By", 2, 1, 2), ("F", 3), ("Bx", 0, -1, -2), ("By", 0, -1, 4), ("By", 0, 1, 4),
+    ("By2", 0, -1, -3), ("sB0", 0), ("By2", 2, -1, -2), ("Bx", 2, 1, 0), ("By", 2, 1, -2), ("By", 2, -1, -3),
+    ("Bx", 1, -1, -2), ("Bz", 2, 4, 1), ("sAz", 0, 3, 1), ("Az", 0, 4, 1, None), ("Az", 3, 1, 1, 0),
+    ("Az", 3, 1, -1, 3), ("Az", 3, 2, -1, 0), ("By", 1, -1, 4), ("sB0", 1), ("By", 1, 1, 4),
+    ("sAz", 2, 3, -1), ("By2", 1, -1, -3), ("Az", 3, 1, 1, 1), ("Az", 2, 4, -1, None), ("Bx", 0, 1, 3),
+    ("By2", 2, 1, 1), ("Az", 3, 1, 1, 2), ("Bx", 1, 1, 3), ("sAz", 1, 3, 1), ("By", 2, 1, 3),
+    ("Az", 3, 2, -1, 1), ("By2", 0, -1, 4), ("sBy", 0, -1), ("Az", 1, 4, 1, None), ("sAz", 2, 3, 1),
+    ("By", 2, 1, -3), ("Bx", 0, -1, -3), ("By", 2, -1, 4), ("sB0", 2), ("Bx", 2, -1, -2),
+    ("Az", 2, 4, 1, None), ("Az", 3, 2, -1, 2), ("By2", 2, 1, 2), ("sA4", 0), ("Az", 3, 1, 1, 3),
+    ("By", 2, 1, 4), ("By2", 2, -1, -3), ("sBy", 0, 1), ("sAz", 3, 1, -1), ("Az", 3, 2, -1, 3),
+    ("Az", 3, 2, 1, 0), ("By2", 1, -1, 4), ("sBy", 1, -1), ("Bx", 1, -1, -3), ("Az", 3, 3, -1, 0),
+    ("Bx", 0, -1, 4), ("sBy", 1, 1), ("Az", 3, 2, 1, 1), ("Bx", 2, 1, 1), ("By2", 2, -1, 4), ("sBy", 2, -1),
+    ("Bx", 2, -1, -3), ("By2", 2, 1, 3), ("Az", 3, 2, 1, 2), ("Az", 3, 3, -1, 1), ("Bx", 1, -1, 4),
+    ("sB2", 0), ("sA4", 1), ("sA4", 2), ("Az", 3, 3, -1, 2), ("Bx", 2, 1, 2), ("Bx", 2, -1, 4), ("sBy", 2, 1),
+    ("sB2", 1), ("sAz", 3, 1, 1), ("sAz", 3, 2, -1), ("Az", 3, 2, 1, 3), ("Az", 3, 3, -1, 3), ("Bx", 2, 1, 3),
+    ("PJ", 0), ("Az", 3, 3, 1, 0), ("sB2", 2), ("BW", 0), ("Az", 3, 3, 1, 1), ("PJ", 1), ("Az", 3, 3, 1, 2),
+    ("Az", 3, 4, -1, 2), ("sAz", 3, 2, 1), ("sAz", 3, 3, -1), ("Az", 3, 3, 1, 3), ("Az", 3, 4, -1, 3),
+    ("PJ", 2), ("Az", 3, 4, 1, 0), ("PZ", 3, 0, 1), ("PZ", 3, 1, 1), ("Az", 3, 4, 1, 1), ("PZ", 3, 1, -1),
+    ("PZ", 3, 2, 1), ("PZ", 3, 2, -1), ("PZ", 3, 3, -1), ("BW", 1), ("BW", 2), ("sAz", 3, 3, 1), ("sA4", 3),
+    ("PZ", 3, 3, 1), ("PZ", 3, 4, 1), ("BW", 3),
 ]
 
 
@@ -103,9 +108,9 @@
 def kernel(
     q_ref, k_ref, v_ref, win_ref, w_ref, go_ref,
     out_ref, gq_ref, gk_ref, gv_ref,
-    G, kv, go_other, dist, probs, attn, ga, acc, out_send, out_recv, ds_buf, pl_buf, own,
+    G, kv, go_other, dist, probs, attn, ga, acc, out_send, out_recv, ds_buf, pl_buf, own, near_own,
     g_send, g_recv, sinks, sink_r1, sink_r2,
-    send_sems, recv_sems, local_sems, tree_send, tree_recv,
+    send_sems, recv_sems, local_sems, tree_send, tree_recv, pair_send, pair_recv,
 ):
     s, hd = lax.axis_index("seq"), lax.axis_index("head")
     c, x, z, y = s % 2, (s // 2) % 2, (s // 4) % NZ, s // (4 * NZ)
@@ -188,6 +193,7 @@
     own_kv = kv.at[:, pl.ds(2 * SLAB, SLAB)]
     first16 = kv.at[:, pl.ds(2 * SLAB, 16)]
     sink_kv = kv.at[:, pl.ds(3 * SLAB, 16)]
+    near_kv, far_kv = kv.at[:, pl.ds(SLAB, SLAB)], kv.at[:, pl.ds(0, SLAB)]
 
     def tree_copy(src, slot, rslot, device):
         return pltpu.make_async_remote_copy(
@@ -280,12 +286,39 @@
     plus = (0, 1, 2, 3)
 
     def near():
-        start("near", own_kv, kv.at[:, pl.ds(SLAB, SLAB)], after1)
+        need(("x", STAGES - 1))
+        start("near", own_kv, near_kv, after1)
+
+    def far_copy(src, slot, device):
+        return pltpu.make_async_remote_copy(
+            src_ref=src, dst_ref=far_kv, send_sem=pair_send.at[slot], recv_sem=pair_recv.at[0],
+            device_id=device, device_id_type=MESH)
 
     def far():
-        start("far", own_kv, kv.at[:, pl.ds(0, SLAB)], after2)
+        @pl.when(c == 0)
+        def _():
+            far_copy(own_kv, 0, after2).start()
+
+    def far2():
+        need("near")
+
+        @pl.when(c == 0)
+        def _():
+            far_copy(near_kv, 1, sib).start()
+
+    def have_halo():
+        need("near")
+        if "far" not in ready:
+            ready.add("far")
+            far_copy(own_kv, 0, sib).wait_recv()
+
+            @pl.when(c == 0)
+            def _():
+                far_copy(own_kv, 0, after2).wait_send()
+                far_copy(near_kv, 1, sib).wait_send()
 
     def go(i):
+        need("near")
         piece = pl.ds(i * 512, 512)
         start(("go", i), go_ref.at[:, piece], go_other.at[:, piece], pair)
 
@@ -340,7 +373,11 @@
 
     def By2(h, d, r):
         need(("By", h, d, r))
-        push(("By2", h, d, r), block(h, False, one(ym(-d)), one(zm(r))), y_dev[d])
+        push(("By2", h, d, r), block(h, False, one(ym(-d)), one(zm(r)), one(x)), y_dev[d])
+
+    def Bx(h, d, r):
+        need(("By2", h, d, r))
+        push(("Bx", h, d, r), block(h, False, one(ym(2)), one(zm(r)), one(x)), x_dev)
 
     def sB0(h):
         for r in range(-3, 5):
@@ -352,7 +389,8 @@
         push(("sBy", h, d), block(h, False, one(ym(-d)), all_z), sib)
 
     def sB2(h):
-        need(*[("By2", h, 1 if r in plus else -1, r) for r in range(-3, 5)])
+        for name in ("By2", "Bx"):
+            need(*[(name, h, 1 if r in plus else -1, r) for r in range(-3, 5)])
         push(("sB2", h), block(h, False, one(ym(2)), all_z), sib)
 
     def gathered(h):
@@ -370,7 +408,7 @@
         dist[...] = jnp.where(band, gap, jnp.where(sink, 0, FAR_AWAY))
 
     def forward(h):
-        need("near", "far")
+        have_halo()
         keys, vals = kv[0, :, h * HEAD : (h + 1) * HEAD], kv[1, :, h * HEAD : (h + 1) * HEAD]
         for j in range(4 * h, 4 * h + 4):
             cols = slice(j * HEAD, (j + 1) * HEAD)
@@ -396,7 +434,7 @@
                     acc[half, yy, z0 + i] = part if h == 0 else acc[half, yy, z0 + i] + part
                 cols = slice(k * 512, (k + 1) * 512)
                 g = dot((go_ref if half == 0 else go_other)[:, cols], w, 1, 0)
-                ga[...] = g if half == 0 and k == 0 else ga[...] + g
+                ga[h] = g if half == 0 and k == 0 else ga[h] + g
 
     def out_lanes(yy, zz):
         return pl.ds(pl.multiple_of(yy * 1024 + zz * 128, 128), 128)
@@ -425,14 +463,14 @@
             side = go_ref if half == 0 else go_other
             cols = jnp.concatenate([side[:, out_lanes(0, zz)], side[:, out_lanes(1, zz)]], axis=1)
             g = dot(cols, w, 1, 0)
-            ga[...] = g if n == 0 and half == 1 else ga[...] + g
+            ga[h] = g if n == 0 and half == 1 else ga[h] + g
 
     def backward(h):
         keys, vals = kv[0, :, h * HEAD : (h + 1) * HEAD], kv[1, :, h * HEAD : (h + 1) * HEAD]
         for i in range(4):
             j = 4 * h + i
             cols = slice(j * HEAD, (j + 1) * HEAD)
-            g = ga[:, i * HEAD : (i + 1) * HEAD].astype(jnp.bfloat16)
+            g = ga[h, :, i * HEAD : (i + 1) * HEAD].astype(jnp.bfloat16)
             delta = jnp.sum(
                 g.astype(jnp.float32) * attn[:, cols].astype(jnp.float32), axis=1, keepdims=True
             )
@@ -441,7 +479,7 @@
             gq_ref[:, cols] = dot(ds, keys, 1, 0).astype(jnp.bfloat16)
             ds_buf[i * SLAB : (i + 1) * SLAB, :] = ds
             pl_buf[i * SLAB : (i + 1) * SLAB, :] = p.astype(jnp.bfloat16)
-        g4 = jnp.concatenate([ga[:, i * HEAD : (i + 1) * HEAD] for i in range(4)], axis=0)
+        g4 = jnp.concatenate([ga[h, :, i * HEAD : (i + 1) * HEAD] for i in range(4)], axis=0)
         q4 = jnp.concatenate(
             [q_ref[:, (4 * h + i) * HEAD : (4 * h + i + 1) * HEAD] for i in range(4)], axis=0
         )
@@ -450,76 +488,136 @@
         dv = dot(pl_buf[...], g4.astype(jnp.bfloat16), 0, 0)
         for i, d in enumerate((dk, dv)):
             g_send[h, 0, i] = d[:SLAB].astype(jnp.bfloat16)
-            g_send[h, 1, i] = d[SLAB : 2 * SLAB].astype(jnp.bfloat16)
             own[i, :, lane] = d[2 * SLAB : 3 * SLAB]
         upper = lax.broadcasted_iota(jnp.int32, (8, HEAD), 0) < SINKS
         sinks[:, lane] = jnp.where(
             upper, dk[3 * SLAB : 3 * SLAB + 8], pltpu.roll(dv[3 * SLAB : 3 * SLAB + 8], SINKS, 0)
         )
-        start(("gfar", h), g_send.at[h, 0], g_recv.at[h, 0], before2)
+        far_grad(h).start()
+
+        for i, d in enumerate((dk, dv)):
+            near_own[h, i] = d[SLAB : 2 * SLAB]
+
+    def send_near(h):
+        @pl.when(c == 0)
+        def _():
+            arrived(h, 1).wait_recv()
+            g_send[h, 1] = (near_own[h] + g_recv[h, 2].astype(jnp.float32)).astype(jnp.bfloat16)
+
+        @pl.when(c != 0)
+        def _():
+            g_send[h, 1] = near_own[h].astype(jnp.bfloat16)
+
         start(("gnear", h), g_send.at[h, 1], g_recv.at[h, 1], before1)
 
-    def up(dst, slot, device):
+    far_owner = (jnp.where(c == 0, before2[0], sib[0]), hd)
+
+    def far_grad(h):
         return pltpu.make_async_remote_copy(
-            src_ref=sinks, dst_ref=dst, send_sem=tree_send.at[14], recv_sem=tree_recv.at[1 + slot],
-            device_id=device, device_id_type=MESH)
-
-    def collect():
-        @pl.when(quad != 0)
-        def _():
-            copy = up(sink_r1.at[quad - 1], quad - 1, at(y, z, 0, 0))
-            copy.start()
-            copy.wait_send()
-
-        @pl.when(leader)
-        def _():
-            for k in range(3):
-                up(sink_r1.at[k], k, sib).wait_recv()
-            sinks[...] = sinks[...] + sink_r1[0] + sink_r1[1] + sink_r1[2]
-
-            @pl.when(place != 0)
-            def _():
-                copy = up(sink_r2.at[place - 1], 2 + place, at(0, 0, 0, 0))
-                copy.start()
-                copy.wait_send()
-
-            @pl.when(place == 0)
-            def _():
-                total = sinks[...]
+            src_ref=g_send.at[h, 0], dst_ref=g_recv.at[h, 2 * c], send_sem=pair_send.at[2 + h],
+            recv_sem=pair_recv.at[1 + 2 * h + c], device_id=far_owner, device_id_type=MESH)
+
+    def arrived(h, from_core):
+        return pltpu.make_async_remote_copy(
+            src_ref=g_send.at[h, 0], dst_ref=g_recv.at[h, 2 * from_core], send_sem=pair_send.at[2 + h],
+            recv_sem=pair_recv.at[1 + 2 * h + from_core], device_id=sib, device_id_type=MESH)
+
+    parts = (pl.ds(0, 384), pl.ds(384, 128))
+
+    def up(part, dst, slot, device):
+        lane = parts[part]
+        return pltpu.make_async_remote_copy(
+            src_ref=sinks.at[:, lane], dst_ref=dst.at[:, lane], send_sem=tree_send.at[14 + part],
+            recv_sem=tree_recv.at[1 + 34 * part + slot], device_id=device, device_id_type=MESH)
+
+    def collect(part, level):
+        lane = slice(384 * part, 384 + 128 * part)
+        if level == 0:
+
+            @pl.when(quad != 0)
+            def _():
+                up(part, sink_r1.at[quad - 1], quad - 1, at(y, z, 0, 0)).start()
+
+        if level == 1:
+
+            @pl.when(leader)
+            def _():
+                total = sinks[:, lane]
+                for k in range(3):
+                    up(part, sink_r1.at[k], k, sib).wait_recv()
+                    total = total + sink_r1[k, :, lane]
+                sinks[:, lane] = total
+
+            @pl.when(leader & (place != 0))
+            def _():
+                up(part, sink_r2.at[place - 1], 2 + place, at(0, 0, 0, 0)).start()
+
+        if level == 2:
+
+            @pl.when(root)
+            def _():
+                total = sinks[:, lane]
                 for k in range(NY * NZ - 1):
-                    up(sink_r2.at[k], 3 + k, sib).wait_recv()
-                    total = total + sink_r2[k]
-                keep = lax.broadcasted_iota(jnp.int32, (8, 512), 0) < SINKS
-                own[0, 0:8, :] = own[0, 0:8, :] + jnp.where(keep, total, 0.0)
-                own[1, 0:8, :] = own[1, 0:8, :] + jnp.where(keep, pltpu.roll(total, SINKS, 0), 0.0)
+                    up(part, sink_r2.at[k], 3 + k, sib).wait_recv()
+                    total = total + sink_r2[k, :, lane]
+                keep = lax.broadcasted_iota(jnp.int32, total.shape, 0) < SINKS
+                low = jnp.where(keep, pltpu.roll(total, SINKS, 0), 0.0)
+                own[0, 0:8, lane] = own[0, 0:8, lane] + jnp.where(keep, total, 0.0)
+                own[1, 0:8, lane] = own[1, 0:8, lane] + low
+
+            @pl.when(jnp.logical_not(root))
+            def _():
+                up(part, sink_r1.at[0], 0, sib).wait_send()
 
     sent = []
-    act = dict(x=x_, near=near, far=far, go=go, Ay=Ay, Az=Az, sA0=sA0, sAz=sAz, sA4=sA4, Bz=Bz, By=By,
-               By2=By2, sB0=sB0, sBy=sBy, sB2=sB2, S=spread, F=forward, PJ=project, PZ=project_z, BW=backward)
+    act = dict(x=x_, near=near, far=far, far2=far2, go=go, Ay=Ay, Az=Az, sA0=sA0, sAz=sAz, sA4=sA4, Bz=Bz, By=By,
+               By2=By2, Bx=Bx, sB0=sB0, sBy=sBy, sB2=sB2, S=spread, F=forward, PJ=project, PZ=project_z, BW=backward)
     spread(0)
     masks()
     for name, *where in ORDER:
+        if name == "PZ" and where[1] == 4:
+            collect(0, 0)
+            for h in range(STAGES - 1):
+                send_near(h)
+            collect(0, 1)
         act[name](*where)
-    collect()
-    for h in range(STAGES):
-        need(("gnear", h), ("gfar", h))
-        lane = slice(h * HEAD, (h + 1) * HEAD)
-        for i, ref in enumerate((gk_ref, gv_ref)):
-            total = own[i, :, lane] + g_recv[h, 0, i].astype(jnp.float32)
-            ref[:, lane] = (total + g_recv[h, 1, i].astype(jnp.float32)).astype(jnp.bfloat16)
+    collect(1, 0)
+    send_near(STAGES - 1)
+    collect(1, 1)
+    collect(0, 2)
     for n, zz in enumerate(sent):
         need(("out", n))
         for yy in range(2):
             total = acc[0, yy, zz] + out_recv[n, yy].astype(jnp.float32)
             out_ref[:, out_lanes(yy, zz)] = total.astype(jnp.bfloat16)
+    collect(1, 2)
+    for h in range(STAGES):
+        need(("gnear", h))
+        far_grad(h).wait_send()
+        lane = slice(h * HEAD, (h + 1) * HEAD)
+
+        @pl.when(c == 0)
+        def _():
+            arrived(h, 0).wait_recv()
+            for i in range(2):
+                own[i, :, lane] = own[i, :, lane] + g_recv[h, 0, i].astype(jnp.float32)
+
+        for i, ref in enumerate((gk_ref, gv_ref)):
+            total = own[i, :, lane] + g_recv[h, 1, i].astype(jnp.float32)
+            ref[:, lane] = total.astype(jnp.bfloat16)
     links.finish()
+
+
+def hand_over(*refs):
+    for src, dst in zip(refs[:4], refs[4:], strict=True):
+        dst[...] = src[...]
 
 
 def local(queries, keys, values, windows, out_weight, grad_out):
     vmem = pl.BlockSpec(memory_space=pltpu.VMEM)
     bf, f32 = jnp.bfloat16, jnp.float32
-    n_copies = 256
-    return pl.pallas_call(
+    n_copies = 288
+    results = pl.pallas_call(
         kernel,
         out_shape=(
             jax.ShapeDtypeStruct((SLAB, 2048), bf),
@@ -536,28 +634,37 @@
             pltpu.VMEM((SLAB, 4 * SLAB), jnp.int32),
             pltpu.VMEM((16, SLAB, 4 * SLAB), f32),
             pltpu.VMEM((SLAB, 2048), bf),
-            pltpu.VMEM((SLAB, 512), f32),
+            pltpu.VMEM((STAGES, SLAB, 512), f32),
             pltpu.VMEM((2, 2, NZ, SLAB, HEAD), f32),
             pltpu.VMEM((NZ, 2, SLAB, HEAD), bf),
             pltpu.VMEM((NZ, 2, SLAB, HEAD), bf),
             pltpu.VMEM((4 * SLAB, 4 * SLAB), bf),
             pltpu.VMEM((4 * SLAB, 4 * SLAB), bf),
             pltpu.VMEM((2, SLAB, 512), f32),
+            pltpu.VMEM((STAGES, 2, SLAB, HEAD), f32),
             pltpu.VMEM((STAGES, 2, 2, SLAB, HEAD), bf),
-            pltpu.VMEM((STAGES, 2, 2, SLAB, HEAD), bf),
+            pltpu.VMEM((STAGES, 3, 2, SLAB, HEAD), bf),
             pltpu.VMEM((8, 512), f32),
             pltpu.VMEM((3, 8, 512), f32),
             pltpu.VMEM((NY * NZ - 1, 8, 512), f32),
             pltpu.SemaphoreType.DMA((n_copies,)),
             pltpu.SemaphoreType.DMA((n_copies,)),
             pltpu.SemaphoreType.DMA((STAGES,)),
-            pltpu.SemaphoreType.DMA((15,)),
-            pltpu.SemaphoreType.DMA((3 + NY * NZ,)),
+            pltpu.SemaphoreType.DMA((16,)),
+            pltpu.SemaphoreType.DMA((1 + 2 * 34,)),
+            pltpu.SemaphoreType.DMA((2 + STAGES,)),
+            pltpu.SemaphoreType.DMA((1 + 2 * STAGES,)),
         ],
         compiler_params=pltpu.CompilerParams(
             collective_id=0, has_side_effects=True, vmem_limit_bytes=58 << 20
         ),
     )(queries, keys, values, windows, out_weight.T, grad_out)
+    return pl.pallas_call(
+        hand_over,
+        out_shape=tuple(jax.ShapeDtypeStruct(r.shape, r.dtype) for r in results),
+        in_specs=[vmem] * 4,
+        out_specs=(vmem,) * 4,
+    )(*results)
 
 
 def solution(mesh):

time: 106 us -> 98.9 us (0.933)
  local copies, waits for them, and re-layouts: 4.57 us -> 0 us
  Pallas kernels: 101 us -> 98.1 us
    pallas_call x1, Pallas kernels: 101 us -> 95.8 us  [local(): pl.pallas_call(kernel, out_shape=(jax.ShapeDtypeStruct((SLAB, 2048), bf),...]
    unnamed x10 -> x0, local copies, waits for them, and re-layouts: 4.57 us -> none
    pallas_call x0 -> x1, Pallas kernels: none -> 2.34 us  [local(): pl.pallas_call(hand_over, out_shape=tuple((jax.ShapeDtypeStruct(r.shape,...]
where the time goes in v3:
time: 98.9 us; the launch traced here: 98.8 us
  Pallas kernels  98.1 us (99%)
    pallas_call x1, Pallas kernels, local(): pl.pallas_call(kernel, out_shape=(jax.ShapeDtypeStruct((SLAB, 2048), bf),...  95.8 us
    pallas_call x1, Pallas kernels, local(): pl.pallas_call(hand_over, out_shape=tuple((jax.ShapeDtypeStruct(r.shape,...  2.34 us

profile of v3, /device:TPU:4, one launch (start us, length us, event | category | flops | bytes accessed | tf_op | source)
XLA Modules:
  0.0 98.8 jit_solution(4223386717193967403)
XLA Ops:
  0.6 95.8 %shard_map.93 = (bf16[128,2048]{1,0:T(8,128)(2,1)}, bf16[128,2048]{1,0:T(8,128)(2,1)}, bf16[128,512]{1,0:T(8,128)(2,1)}, bf16[128,512]{1,0:T(8,128)(2,1)}) custom-call(bf16[128,2048]{1,0:T(8,128)(2,1)} %q_ref.1, bf16[128,512]{1,0:T(8,128)(2,1)} %k_ref.1, bf16[128,512]{1,0:T(8,128)(2,1)} %v_ref.1, s32[16]{0:T(128)} %win_ref.1, bf16[32,2048]{1,0:T(8,128)(2,1)} %bitcast.1, ...), custom_call_target="tpu_custom_call" | custom-call | tf_op jit(solution)/shard_map/pallas_call | solution.py:620
  96.4 2.3 %shard_map.94 = (bf16[128,2048]{1,0:T(8,128)(2,1)}, bf16[128,2048]{1,0:T(8,128)(2,1)}, bf16[128,512]{1,0:T(8,128)(2,1)}, bf16[128,512]{1,0:T(8,128)(2,1)}) custom-call(bf16[128,2048]{1,0:T(8,128)(2,1)} %get-tuple-element.8.refs_0_, bf16[128,2048]{1,0:T(8,128)(2,1)} %get-tuple-element.9.refs_1_, bf16[128,512]{1,0:T(8,128)(2,1)} %get-tuple-element.10.refs_2_, ...), custom_call_target="tpu_custom_call" | custom-call | tf_op jit(solution)/shard_map/pallas_call | solution.py:662

commit v4 on v3

--- a/solution.py
+++ b/solution.py
@@ -27,36 +27,36 @@
     ("Ay", 2, 2), ("By", 2, 1, 0), ("By", 2, -1, 0), ("Bz", 2, 1, 1), ("Bz", 2, 1, -1), ("near",), ("far",),
     ("Ay", 3, 1), ("Ay", 3, -1), ("Ay", 3, 2), ("sA0", 0), ("Az", 0, 1, -1, None), ("Bz", 0, 2, -1),
     ("By", 0, -1, -1), ("Bz", 1, 2, -1), ("sA0", 1), ("Az", 1, 1, -1, None), ("By", 0, -1, 1),
-    ("Bz", 2, 2, -1), ("Bz", 0, 2, 1), ("By", 1, -1, -1), ("By2", 0, 1, 0), ("By", 0, 1, 1), ("S", 1),
-    ("far2",), ("Az", 0, 1, 1, None), ("sA0", 2), ("By", 1, -1, 1), ("sAz", 0, 1, -1), ("Az", 0, 2, -1, None),
+    ("Bz", 2, 2, -1), ("Bz", 0, 2, 1), ("By", 1, -1, -1), ("By2", 0, 1, 0), ("By", 0, 1, 1), ("far2",),
+    ("Az", 0, 1, 1, None), ("sA0", 2), ("By", 1, -1, 1), ("sAz", 0, 1, -1), ("Az", 0, 2, -1, None),
     ("By", 0, 1, -1), ("Az", 2, 1, -1, None), ("By", 2, -1, -1), ("Bz", 1, 2, 1), ("By", 0, 1, 2),
     ("Bz", 0, 3, -1), ("By", 0, -1, 2), ("Az", 1, 1, 1, None), ("go", 0), ("go", 1), ("go", 2),
-    ("By2", 1, 1, 0), ("go", 3), ("Bz", 1, 3, -1), ("By", 1, 1, 1), ("By", 1, -1, 2), ("sAz", 1, 1, -1),
-    ("Az", 2, 1, 1, None), ("Az", 1, 2, -1, None), ("By2", 0, -1, -1), ("S", 2), ("By", 1, 1, -1), ("sA0", 3),
-    ("By", 2, -1, 1), ("Bx", 0, 1, 0), ("Bz", 2, 2, 1), ("By", 1, 1, 2), ("Bz", 2, 3, -1), ("By", 0, -1, -2),
-    ("sAz", 0, 2, -1), ("Bz", 0, 3, 1), ("By2", 0, 1, 1), ("Az", 0, 3, -1, None), ("sAz", 0, 1, 1),
-    ("By2", 1, -1, -1), ("By", 0, 1, -2), ("Az", 0, 2, 1, None), ("By", 2, -1, 2), ("sAz", 2, 1, -1),
-    ("By", 1, 1, -2), ("Az", 2, 2, -1, None), ("By", 1, -1, -2), ("Bz", 1, 3, 1), ("Bx", 1, 1, 0),
-    ("By2", 0, 1, 2), ("sAz", 1, 1, 1), ("Bz", 0, 4, -1), ("By", 0, 1, 3), ("By", 0, -1, 3),
-    ("Az", 1, 2, 1, None), ("S", 3), ("F", 0), ("Bx", 0, -1, -1), ("By2", 1, 1, 1), ("sAz", 1, 2, -1),
-    ("By", 1, 1, 3), ("By", 1, -1, 3), ("Bz", 1, 4, -1), ("Az", 1, 3, -1, None), ("By2", 2, -1, -1),
-    ("sAz", 2, 1, 1), ("Az", 2, 2, 1, None), ("Bz", 2, 4, -1), ("By2", 1, 1, 2), ("By", 2, -1, -2),
-    ("Bx", 0, 1, 1), ("Az", 3, 1, -1, 0), ("Bz", 2, 3, 1), ("F", 1), ("By2", 0, -1, -2), ("sAz", 0, 2, 1),
-    ("sAz", 0, 3, -1), ("Bz", 0, 4, 1), ("By", 0, -1, -3), ("By", 0, 1, -3), ("Az", 0, 3, 1, None),
-    ("Az", 0, 4, -1, None), ("Bx", 1, -1, -1), ("By2", 2, 1, 0), ("Bx", 0, 1, 2), ("By2", 1, -1, -2),
-    ("By", 1, 1, -3), ("sAz", 2, 2, -1), ("By", 1, -1, -3), ("By", 2, 1, 1), ("Bz", 1, 4, 1),
-    ("Az", 2, 3, -1, None), ("F", 2), ("By2", 0, 1, 3), ("Bx", 1, 1, 1), ("sAz", 1, 2, 1), ("sAz", 1, 3, -1),
-    ("Az", 1, 3, 1, None), ("Az", 1, 4, -1, None), ("By2", 1, 1, 3), ("Bx", 2, -1, -1), ("By", 2, 1, -1),
-    ("By", 2, -1, 3), ("sAz", 2, 2, 1), ("Az", 2, 3, 1, None), ("Bx", 1, 1, 2), ("Az", 3, 1, -1, 1),
-    ("Az", 3, 1, -1, 2), ("By", 2, 1, 2), ("F", 3), ("Bx", 0, -1, -2), ("By", 0, -1, 4), ("By", 0, 1, 4),
+    ("By2", 1, 1, 0), ("go", 3), ("S", 1), ("Bz", 1, 3, -1), ("By", 1, 1, 1), ("By", 1, -1, 2),
+    ("sAz", 1, 1, -1), ("Az", 2, 1, 1, None), ("Az", 1, 2, -1, None), ("By2", 0, -1, -1), ("By", 1, 1, -1),
+    ("sA0", 3), ("By", 2, -1, 1), ("Bx", 0, 1, 0), ("Bz", 2, 2, 1), ("By", 1, 1, 2), ("Bz", 2, 3, -1),
+    ("By", 0, -1, -2), ("sAz", 0, 2, -1), ("Bz", 0, 3, 1), ("By2", 0, 1, 1), ("Az", 0, 3, -1, None),
+    ("sAz", 0, 1, 1), ("By2", 1, -1, -1), ("By", 0, 1, -2), ("Az", 0, 2, 1, None), ("By", 2, -1, 2),
+    ("sAz", 2, 1, -1), ("By", 1, 1, -2), ("Az", 2, 2, -1, None), ("By", 1, -1, -2), ("Bz", 1, 3, 1),
+    ("Bx", 1, 1, 0), ("By2", 0, 1, 2), ("sAz", 1, 1, 1), ("Bz", 0, 4, -1), ("By", 0, 1, 3), ("By", 0, -1, 3),
+    ("Az", 1, 2, 1, None), ("Bx", 0, -1, -1), ("By2", 1, 1, 1), ("sAz", 1, 2, -1), ("By", 1, 1, 3),
+    ("By", 1, -1, 3), ("Bz", 1, 4, -1), ("Az", 1, 3, -1, None), ("By2", 2, -1, -1), ("sAz", 2, 1, 1),
+    ("Az", 2, 2, 1, None), ("Bz", 2, 4, -1), ("By2", 1, 1, 2), ("S", 2), ("By", 2, -1, -2), ("Bx", 0, 1, 1),
+    ("Az", 3, 1, -1, 0), ("Bz", 2, 3, 1), ("By2", 0, -1, -2), ("sAz", 0, 2, 1), ("sAz", 0, 3, -1),
+    ("Bz", 0, 4, 1), ("By", 0, -1, -3), ("By", 0, 1, -3), ("Az", 0, 3, 1, None), ("Az", 0, 4, -1, None),
+    ("Bx", 1, -1, -1), ("By2", 2, 1, 0), ("Bx", 0, 1, 2), ("By2", 1, -1, -2), ("By", 1, 1, -3),
+    ("sAz", 2, 2, -1), ("By", 1, -1, -3), ("By", 2, 1, 1), ("Bz", 1, 4, 1), ("Az", 2, 3, -1, None),
+    ("By2", 0, 1, 3), ("Bx", 1, 1, 1), ("sAz", 1, 2, 1), ("sAz", 1, 3, -1), ("Az", 1, 3, 1, None),
+    ("Az", 1, 4, -1, None), ("By2", 1, 1, 3), ("Bx", 2, -1, -1), ("By", 2, 1, -1), ("By", 2, -1, 3),
+    ("sAz", 2, 2, 1), ("Az", 2, 3, 1, None), ("Bx", 1, 1, 2), ("Az", 3, 1, -1, 1), ("Az", 3, 1, -1, 2),
+    ("By", 2, 1, 2), ("Bx", 0, -1, -2), ("By", 0, -1, 4), ("S", 3), ("F", 0), ("By", 0, 1, 4),
     ("By2", 0, -1, -3), ("sB0", 0), ("By2", 2, -1, -2), ("Bx", 2, 1, 0), ("By", 2, 1, -2), ("By", 2, -1, -3),
     ("Bx", 1, -1, -2), ("Bz", 2, 4, 1), ("sAz", 0, 3, 1), ("Az", 0, 4, 1, None), ("Az", 3, 1, 1, 0),
-    ("Az", 3, 1, -1, 3), ("Az", 3, 2, -1, 0), ("By", 1, -1, 4), ("sB0", 1), ("By", 1, 1, 4),
+    ("Az", 3, 1, -1, 3), ("Az", 3, 2, -1, 0), ("F", 1), ("By", 1, -1, 4), ("sB0", 1), ("By", 1, 1, 4),
     ("sAz", 2, 3, -1), ("By2", 1, -1, -3), ("Az", 3, 1, 1, 1), ("Az", 2, 4, -1, None), ("Bx", 0, 1, 3),
     ("By2", 2, 1, 1), ("Az", 3, 1, 1, 2), ("Bx", 1, 1, 3), ("sAz", 1, 3, 1), ("By", 2, 1, 3),
-    ("Az", 3, 2, -1, 1), ("By2", 0, -1, 4), ("sBy", 0, -1), ("Az", 1, 4, 1, None), ("sAz", 2, 3, 1),
+    ("Az", 3, 2, -1, 1), ("F", 2), ("By2", 0, -1, 4), ("sBy", 0, -1), ("Az", 1, 4, 1, None), ("sAz", 2, 3, 1),
     ("By", 2, 1, -3), ("Bx", 0, -1, -3), ("By", 2, -1, 4), ("sB0", 2), ("Bx", 2, -1, -2),
-    ("Az", 2, 4, 1, None), ("Az", 3, 2, -1, 2), ("By2", 2, 1, 2), ("sA4", 0), ("Az", 3, 1, 1, 3),
+    ("Az", 2, 4, 1, None), ("Az", 3, 2, -1, 2), ("By2", 2, 1, 2), ("sA4", 0), ("Az", 3, 1, 1, 3), ("F", 3),
     ("By", 2, 1, 4), ("By2", 2, -1, -3), ("sBy", 0, 1), ("sAz", 3, 1, -1), ("Az", 3, 2, -1, 3),
     ("Az", 3, 2, 1, 0), ("By2", 1, -1, 4), ("sBy", 1, -1), ("Bx", 1, -1, -3), ("Az", 3, 3, -1, 0),
     ("Bx", 0, -1, 4), ("sBy", 1, 1), ("Az", 3, 2, 1, 1), ("Bx", 2, 1, 1), ("By2", 2, -1, 4), ("sBy", 2, -1),

time: 98.9 us -> 97.2 us (0.983)
  Pallas kernels: 98.1 us -> 96.4 us
    pallas_call x1, Pallas kernels: 95.8 us -> 94.1 us  [local(): pl.pallas_call(kernel, out_shape=(jax.ShapeDtypeStruct((SLAB, 2048), bf),...]
where the time goes in v4:
time: 97.2 us; the launch traced here: 97 us
  Pallas kernels  96.4 us (99%)
    pallas_call x1, Pallas kernels, local(): pl.pallas_call(kernel, out_shape=(jax.ShapeDtypeStruct((SLAB, 2048), bf),...  94.1 us
    pallas_call x1, Pallas kernels, local(): pl.pallas_call(hand_over, out_shape=tuple((jax.ShapeDtypeStruct(r.shape,...  2.34 us

profile of v4, /device:TPU:4, one launch (start us, length us, event | category | flops | bytes accessed | tf_op | source)
XLA Modules:
  0.0 97.0 jit_solution(767168216535949108)
XLA Ops:
  0.6 94.1 %shard_map.93 = (bf16[128,2048]{1,0:T(8,128)(2,1)}, bf16[128,2048]{1,0:T(8,128)(2,1)}, bf16[128,512]{1,0:T(8,128)(2,1)}, bf16[128,512]{1,0:T(8,128)(2,1)}) custom-call(bf16[128,2048]{1,0:T(8,128)(2,1)} %q_ref.1, bf16[128,512]{1,0:T(8,128)(2,1)} %k_ref.1, bf16[128,512]{1,0:T(8,128)(2,1)} %v_ref.1, s32[16]{0:T(128)} %win_ref.1, bf16[32,2048]{1,0:T(8,128)(2,1)} %bitcast.1, ...), custom_call_target="tpu_custom_call" | custom-call | tf_op jit(solution)/shard_map/pallas_call | solution.py:620
  94.7 2.3 %shard_map.94 = (bf16[128,2048]{1,0:T(8,128)(2,1)}, bf16[128,2048]{1,0:T(8,128)(2,1)}, bf16[128,512]{1,0:T(8,128)(2,1)}, bf16[128,512]{1,0:T(8,128)(2,1)}) custom-call(bf16[128,2048]{1,0:T(8,128)(2,1)} %get-tuple-element.8.refs_0_, bf16[128,2048]{1,0:T(8,128)(2,1)} %get-tuple-element.9.refs_1_, bf16[128,512]{1,0:T(8,128)(2,1)} %get-tuple-element.10.refs_2_, ...), custom_call_target="tpu_custom_call" | custom-call | tf_op jit(solution)/shard_map/pallas_call | solution.py:662

commit v5 on v4

--- a/solution.py
+++ b/solution.py
@@ -24,50 +24,50 @@
     ("x", 0), ("x", 1), ("x", 2), ("x", 3), ("Ay", 0, 1), ("Ay", 0, -1), ("Ay", 0, 2), ("Bz", 0, 1, 1),
     ("Bz", 0, 1, -1), ("By", 0, 1, 0), ("By", 0, -1, 0), ("Ay", 1, 1), ("Ay", 1, -1), ("Ay", 1, 2),
     ("By", 1, 1, 0), ("By", 1, -1, 0), ("Bz", 1, 1, 1), ("Bz", 1, 1, -1), ("Ay", 2, 1), ("Ay", 2, -1),
-    ("Ay", 2, 2), ("By", 2, 1, 0), ("By", 2, -1, 0), ("Bz", 2, 1, 1), ("Bz", 2, 1, -1), ("near",), ("far",),
-    ("Ay", 3, 1), ("Ay", 3, -1), ("Ay", 3, 2), ("sA0", 0), ("Az", 0, 1, -1, None), ("Bz", 0, 2, -1),
-    ("By", 0, -1, -1), ("Bz", 1, 2, -1), ("sA0", 1), ("Az", 1, 1, -1, None), ("By", 0, -1, 1),
-    ("Bz", 2, 2, -1), ("Bz", 0, 2, 1), ("By", 1, -1, -1), ("By2", 0, 1, 0), ("By", 0, 1, 1), ("far2",),
-    ("Az", 0, 1, 1, None), ("sA0", 2), ("By", 1, -1, 1), ("sAz", 0, 1, -1), ("Az", 0, 2, -1, None),
-    ("By", 0, 1, -1), ("Az", 2, 1, -1, None), ("By", 2, -1, -1), ("Bz", 1, 2, 1), ("By", 0, 1, 2),
-    ("Bz", 0, 3, -1), ("By", 0, -1, 2), ("Az", 1, 1, 1, None), ("go", 0), ("go", 1), ("go", 2),
-    ("By2", 1, 1, 0), ("go", 3), ("S", 1), ("Bz", 1, 3, -1), ("By", 1, 1, 1), ("By", 1, -1, 2),
+    ("Ay", 2, 2), ("By", 2, 1, 0), ("By", 2, -1, 0), ("Bz", 2, 1, 1), ("Bz", 2, 1, -1), ("Ay", 3, 1),
+    ("Ay", 3, -1), ("Ay", 3, 2), ("sA0", 0), ("Az", 0, 1, -1, None), ("Bz", 0, 2, -1), ("By", 0, -1, -1),
+    ("Bz", 1, 2, -1), ("sA0", 1), ("Az", 1, 1, -1, None), ("By", 0, -1, 1), ("Bz", 2, 2, -1), ("Bz", 0, 2, 1),
+    ("By", 1, -1, -1), ("By2", 0, 1, 0), ("By", 0, 1, 1), ("Az", 0, 1, 1, None), ("sA0", 2), ("By", 1, -1, 1),
+    ("sAz", 0, 1, -1), ("Az", 0, 2, -1, None), ("By", 0, 1, -1), ("Az", 2, 1, -1, None), ("By", 2, -1, -1),
+    ("Bz", 1, 2, 1), ("By", 0, 1, 2), ("Bz", 0, 3, -1), ("By", 0, -1, 2), ("Az", 1, 1, 1, None),
+    ("By2", 1, 1, 0), ("near",), ("S", 1), ("far",), ("Bz", 1, 3, -1), ("By", 1, 1, 1), ("By", 1, -1, 2),
     ("sAz", 1, 1, -1), ("Az", 2, 1, 1, None), ("Az", 1, 2, -1, None), ("By2", 0, -1, -1), ("By", 1, 1, -1),
     ("sA0", 3), ("By", 2, -1, 1), ("Bx", 0, 1, 0), ("Bz", 2, 2, 1), ("By", 1, 1, 2), ("Bz", 2, 3, -1),
     ("By", 0, -1, -2), ("sAz", 0, 2, -1), ("Bz", 0, 3, 1), ("By2", 0, 1, 1), ("Az", 0, 3, -1, None),
     ("sAz", 0, 1, 1), ("By2", 1, -1, -1), ("By", 0, 1, -2), ("Az", 0, 2, 1, None), ("By", 2, -1, 2),
     ("sAz", 2, 1, -1), ("By", 1, 1, -2), ("Az", 2, 2, -1, None), ("By", 1, -1, -2), ("Bz", 1, 3, 1),
-    ("Bx", 1, 1, 0), ("By2", 0, 1, 2), ("sAz", 1, 1, 1), ("Bz", 0, 4, -1), ("By", 0, 1, 3), ("By", 0, -1, 3),
-    ("Az", 1, 2, 1, None), ("Bx", 0, -1, -1), ("By2", 1, 1, 1), ("sAz", 1, 2, -1), ("By", 1, 1, 3),
-    ("By", 1, -1, 3), ("Bz", 1, 4, -1), ("Az", 1, 3, -1, None), ("By2", 2, -1, -1), ("sAz", 2, 1, 1),
-    ("Az", 2, 2, 1, None), ("Bz", 2, 4, -1), ("By2", 1, 1, 2), ("S", 2), ("By", 2, -1, -2), ("Bx", 0, 1, 1),
-    ("Az", 3, 1, -1, 0), ("Bz", 2, 3, 1), ("By2", 0, -1, -2), ("sAz", 0, 2, 1), ("sAz", 0, 3, -1),
-    ("Bz", 0, 4, 1), ("By", 0, -1, -3), ("By", 0, 1, -3), ("Az", 0, 3, 1, None), ("Az", 0, 4, -1, None),
-    ("Bx", 1, -1, -1), ("By2", 2, 1, 0), ("Bx", 0, 1, 2), ("By2", 1, -1, -2), ("By", 1, 1, -3),
-    ("sAz", 2, 2, -1), ("By", 1, -1, -3), ("By", 2, 1, 1), ("Bz", 1, 4, 1), ("Az", 2, 3, -1, None),
-    ("By2", 0, 1, 3), ("Bx", 1, 1, 1), ("sAz", 1, 2, 1), ("sAz", 1, 3, -1), ("Az", 1, 3, 1, None),
-    ("Az", 1, 4, -1, None), ("By2", 1, 1, 3), ("Bx", 2, -1, -1), ("By", 2, 1, -1), ("By", 2, -1, 3),
-    ("sAz", 2, 2, 1), ("Az", 2, 3, 1, None), ("Bx", 1, 1, 2), ("Az", 3, 1, -1, 1), ("Az", 3, 1, -1, 2),
-    ("By", 2, 1, 2), ("Bx", 0, -1, -2), ("By", 0, -1, 4), ("S", 3), ("F", 0), ("By", 0, 1, 4),
-    ("By2", 0, -1, -3), ("sB0", 0), ("By2", 2, -1, -2), ("Bx", 2, 1, 0), ("By", 2, 1, -2), ("By", 2, -1, -3),
-    ("Bx", 1, -1, -2), ("Bz", 2, 4, 1), ("sAz", 0, 3, 1), ("Az", 0, 4, 1, None), ("Az", 3, 1, 1, 0),
-    ("Az", 3, 1, -1, 3), ("Az", 3, 2, -1, 0), ("F", 1), ("By", 1, -1, 4), ("sB0", 1), ("By", 1, 1, 4),
-    ("sAz", 2, 3, -1), ("By2", 1, -1, -3), ("Az", 3, 1, 1, 1), ("Az", 2, 4, -1, None), ("Bx", 0, 1, 3),
-    ("By2", 2, 1, 1), ("Az", 3, 1, 1, 2), ("Bx", 1, 1, 3), ("sAz", 1, 3, 1), ("By", 2, 1, 3),
-    ("Az", 3, 2, -1, 1), ("F", 2), ("By2", 0, -1, 4), ("sBy", 0, -1), ("Az", 1, 4, 1, None), ("sAz", 2, 3, 1),
-    ("By", 2, 1, -3), ("Bx", 0, -1, -3), ("By", 2, -1, 4), ("sB0", 2), ("Bx", 2, -1, -2),
-    ("Az", 2, 4, 1, None), ("Az", 3, 2, -1, 2), ("By2", 2, 1, 2), ("sA4", 0), ("Az", 3, 1, 1, 3), ("F", 3),
-    ("By", 2, 1, 4), ("By2", 2, -1, -3), ("sBy", 0, 1), ("sAz", 3, 1, -1), ("Az", 3, 2, -1, 3),
-    ("Az", 3, 2, 1, 0), ("By2", 1, -1, 4), ("sBy", 1, -1), ("Bx", 1, -1, -3), ("Az", 3, 3, -1, 0),
-    ("Bx", 0, -1, 4), ("sBy", 1, 1), ("Az", 3, 2, 1, 1), ("Bx", 2, 1, 1), ("By2", 2, -1, 4), ("sBy", 2, -1),
-    ("Bx", 2, -1, -3), ("By2", 2, 1, 3), ("Az", 3, 2, 1, 2), ("Az", 3, 3, -1, 1), ("Bx", 1, -1, 4),
-    ("sB2", 0), ("sA4", 1), ("sA4", 2), ("Az", 3, 3, -1, 2), ("Bx", 2, 1, 2), ("Bx", 2, -1, 4), ("sBy", 2, 1),
-    ("sB2", 1), ("sAz", 3, 1, 1), ("sAz", 3, 2, -1), ("Az", 3, 2, 1, 3), ("Az", 3, 3, -1, 3), ("Bx", 2, 1, 3),
-    ("PJ", 0), ("Az", 3, 3, 1, 0), ("sB2", 2), ("BW", 0), ("Az", 3, 3, 1, 1), ("PJ", 1), ("Az", 3, 3, 1, 2),
-    ("Az", 3, 4, -1, 2), ("sAz", 3, 2, 1), ("sAz", 3, 3, -1), ("Az", 3, 3, 1, 3), ("Az", 3, 4, -1, 3),
-    ("PJ", 2), ("Az", 3, 4, 1, 0), ("PZ", 3, 0, 1), ("PZ", 3, 1, 1), ("Az", 3, 4, 1, 1), ("PZ", 3, 1, -1),
-    ("PZ", 3, 2, 1), ("PZ", 3, 2, -1), ("PZ", 3, 3, -1), ("BW", 1), ("BW", 2), ("sAz", 3, 3, 1), ("sA4", 3),
-    ("PZ", 3, 3, 1), ("PZ", 3, 4, 1), ("BW", 3),
+    ("far2",), ("Bx", 1, 1, 0), ("By2", 0, 1, 2), ("sAz", 1, 1, 1), ("Bz", 0, 4, -1), ("By", 0, 1, 3),
+    ("By", 0, -1, 3), ("Az", 1, 2, 1, None), ("Bx", 0, -1, -1), ("By2", 1, 1, 1), ("sAz", 1, 2, -1),
+    ("go", 0), ("By", 1, 1, 3), ("By", 1, -1, 3), ("Bz", 1, 4, -1), ("Az", 1, 3, -1, None),
+    ("By2", 2, -1, -1), ("sAz", 2, 1, 1), ("Az", 2, 2, 1, None), ("Bz", 2, 4, -1), ("By2", 1, 1, 2), ("S", 2),
+    ("go", 1), ("By", 2, -1, -2), ("Bx", 0, 1, 1), ("Az", 3, 1, -1, 0), ("Bz", 2, 3, 1), ("By2", 0, -1, -2),
+    ("sAz", 0, 2, 1), ("sAz", 0, 3, -1), ("Bz", 0, 4, 1), ("By", 0, -1, -3), ("By", 0, 1, -3), ("go", 2),
+    ("Az", 0, 3, 1, None), ("Az", 0, 4, -1, None), ("Bx", 1, -1, -1), ("By2", 2, 1, 0), ("Bx", 0, 1, 2),
+    ("By2", 1, -1, -2), ("By", 1, 1, -3), ("sAz", 2, 2, -1), ("By", 1, -1, -3), ("By", 2, 1, 1), ("go", 3),
+    ("Bz", 1, 4, 1), ("Az", 2, 3, -1, None), ("By2", 0, 1, 3), ("Bx", 1, 1, 1), ("sAz", 1, 2, 1),
+    ("sAz", 1, 3, -1), ("Az", 1, 3, 1, None), ("Az", 1, 4, -1, None), ("By2", 1, 1, 3), ("Bx", 2, -1, -1),
+    ("By", 2, 1, -1), ("By", 2, -1, 3), ("sAz", 2, 2, 1), ("Az", 2, 3, 1, None), ("Bx", 1, 1, 2),
+    ("Az", 3, 1, -1, 1), ("Az", 3, 1, -1, 2), ("By", 2, 1, 2), ("Bx", 0, -1, -2), ("By", 0, -1, 4), ("S", 3),
+    ("F", 0), ("By", 0, 1, 4), ("By2", 0, -1, -3), ("sB0", 0), ("By2", 2, -1, -2), ("Bx", 2, 1, 0),
+    ("By", 2, 1, -2), ("By", 2, -1, -3), ("Bx", 1, -1, -2), ("Bz", 2, 4, 1), ("sAz", 0, 3, 1),
+    ("Az", 0, 4, 1, None), ("Az", 3, 1, 1, 0), ("Az", 3, 1, -1, 3), ("Az", 3, 2, -1, 0), ("F", 1),
+    ("By", 1, -1, 4), ("sB0", 1), ("By", 1, 1, 4), ("sAz", 2, 3, -1), ("By2", 1, -1, -3), ("Az", 3, 1, 1, 1),
+    ("Az", 2, 4, -1, None), ("Bx", 0, 1, 3), ("By2", 2, 1, 1), ("Az", 3, 1, 1, 2), ("Bx", 1, 1, 3),
+    ("sAz", 1, 3, 1), ("By", 2, 1, 3), ("Az", 3, 2, -1, 1), ("F", 2), ("By2", 0, -1, 4), ("sBy", 0, -1),
+    ("Az", 1, 4, 1, None), ("sAz", 2, 3, 1), ("By", 2, 1, -3), ("Bx", 0, -1, -3), ("By", 2, -1, 4),
+    ("sB0", 2), ("Bx", 2, -1, -2), ("Az", 2, 4, 1, None), ("Az", 3, 2, -1, 2), ("By2", 2, 1, 2), ("sA4", 0),
+    ("Az", 3, 1, 1, 3), ("F", 3), ("By", 2, 1, 4), ("By2", 2, -1, -3), ("sBy", 0, 1), ("sAz", 3, 1, -1),
+    ("Az", 3, 2, -1, 3), ("Az", 3, 2, 1, 0), ("By2", 1, -1, 4), ("sBy", 1, -1), ("Bx", 1, -1, -3),
+    ("Az", 3, 3, -1, 0), ("Bx", 0, -1, 4), ("sBy", 1, 1), ("Az", 3, 2, 1, 1), ("Bx", 2, 1, 1),
+    ("By2", 2, -1, 4), ("sBy", 2, -1), ("Bx", 2, -1, -3), ("By2", 2, 1, 3), ("Az", 3, 2, 1, 2),
+    ("Az", 3, 3, -1, 1), ("Bx", 1, -1, 4), ("sB2", 0), ("sA4", 1), ("sA4", 2), ("Az", 3, 3, -1, 2),
+    ("Bx", 2, 1, 2), ("Bx", 2, -1, 4), ("sBy", 2, 1), ("sB2", 1), ("sAz", 3, 1, 1), ("sAz", 3, 2, -1),
+    ("Az", 3, 2, 1, 3), ("Az", 3, 3, -1, 3), ("Bx", 2, 1, 3), ("PJ", 0), ("Az", 3, 3, 1, 0), ("sB2", 2),
+    ("BW", 0), ("Az", 3, 3, 1, 1), ("PJ", 1), ("Az", 3, 3, 1, 2), ("Az", 3, 4, -1, 2), ("sAz", 3, 2, 1),
+    ("sAz", 3, 3, -1), ("Az", 3, 3, 1, 3), ("Az", 3, 4, -1, 3), ("PJ", 2), ("Az", 3, 4, 1, 0),
+    ("PZ", 3, 0, 1), ("PZ", 3, 1, 1), ("Az", 3, 4, 1, 1), ("PZ", 3, 1, -1), ("PZ", 3, 2, 1), ("PZ", 3, 2, -1),
+    ("PZ", 3, 3, -1), ("BW", 1), ("BW", 2), ("sAz", 3, 3, 1), ("sA4", 3), ("PZ", 3, 3, 1), ("PZ", 3, 4, 1),
+    ("BW", 3),
 ]
 
 

time: 97.2 us -> 97 us (level)
  no operation moved by 1% of the time
where the time goes in v5:
time: 97 us; the launch traced here: 96.8 us
  Pallas kernels  96.2 us (99%)
    pallas_call x1, Pallas kernels, local(): pl.pallas_call(kernel, out_shape=(jax.ShapeDtypeStruct((SLAB, 2048), bf),...  93.8 us
    pallas_call x1, Pallas kernels, local(): pl.pallas_call(hand_over, out_shape=tuple((jax.ShapeDtypeStruct(r.shape,...  2.34 us

profile of v5, /device:TPU:4, one launch (start us, length us, event | category | flops | bytes accessed | tf_op | source)
XLA Modules:
  0.0 96.8 jit_solution(124591607294713847)
XLA Ops:
  0.6 93.8 %shard_map.93 = (bf16[128,2048]{1,0:T(8,128)(2,1)}, bf16[128,2048]{1,0:T(8,128)(2,1)}, bf16[128,512]{1,0:T(8,128)(2,1)}, bf16[128,512]{1,0:T(8,128)(2,1)}) custom-call(bf16[128,2048]{1,0:T(8,128)(2,1)} %q_ref.1, bf16[128,512]{1,0:T(8,128)(2,1)} %k_ref.1, bf16[128,512]{1,0:T(8,128)(2,1)} %v_ref.1, s32[16]{0:T(128)} %win_ref.1, bf16[32,2048]{1,0:T(8,128)(2,1)} %bitcast.1, ...), custom_call_target="tpu_custom_call" | custom-call | tf_op jit(solution)/shard_map/pallas_call | solution.py:620
  94.5 2.3 %shard_map.94 = (bf16[128,2048]{1,0:T(8,128)(2,1)}, bf16[128,2048]{1,0:T(8,128)(2,1)}, bf16[128,512]{1,0:T(8,128)(2,1)}, bf16[128,512]{1,0:T(8,128)(2,1)}) custom-call(bf16[128,2048]{1,0:T(8,128)(2,1)} %get-tuple-element.8.refs_0_, bf16[128,2048]{1,0:T(8,128)(2,1)} %get-tuple-element.9.refs_1_, bf16[128,512]{1,0:T(8,128)(2,1)} %get-tuple-element.10.refs_2_, ...), custom_call_target="tpu_custom_call" | custom-call | tf_op jit(solution)/shard_map/pallas_call | solution.py:662
